TPU v7x, 32 devices: a whole 2x2x4 slice. The times are simulated.
32 devices in a mesh: feat: 8 (over y, x, core), samp: 4 (over z).
Axes of the slice: x: 2, y: 2, z: 4, core: 2. Of those that a mesh axis runs over, the one named last changes fastest.
Arguments:
- hash_codes: int32 [8, 3072, 1024], P('feat', 'samp'), may hold values from 0 to 4095
- sample_index: int32 [8, 8192], P('feat', 'samp'), may hold values from 0 to 767, as said below
- labels: int32 [2048, 4], P('feat', 'samp'), may hold values 0 or 1
- encoder_first: bfloat16 [8, 1024, 2048], P('feat'), may hold values from -0.1875 to 0.1875
- encoder_second: bfloat16 [8, 2048, 256], P('feat'), may hold values from -0.125 to 0.125
- top_weight: bfloat16 [64, 1024], replicated, may hold values from -0.75 to 0.75
- score_vector: bfloat16 [1024], replicated, may hold values from -0.1875 to 0.1875
Outputs:
- row_grads: float32 [8, 3072, 256], P('feat', 'samp')
- grad_first: float32 [8, 1024, 2048], P('feat', 'samp')
- grad_second: float32 [8, 2048, 256], P('feat', 'samp')
Inputs may be any that keep to these rules, and one draw needn't show every extreme that they name: `sample_index`: for each feature and sample group the slots used by the group's 2048 samples are 0 to some count minus 1, each at least once; for some feature and group that count is 768.
All inputs are finite; a program needn't handle non-finite values. No bound on the sum of `labels` on one device may be relied on, other than what follows from the above.
Results may differ from a plain program's by a relative error of at most 0.019.
Values may be sent and summed in bfloat16 or wider, within the bound.
A program may use at most 128 MiB of HBM per device.

v0:
```python
import jax
import jax.numpy as jnp
from jax import lax
from jax.sharding import PartitionSpec as P

BUCKETS = 4096


loss_scale = 256.0


def silu_slope(inputs):
    logistic = jax.nn.sigmoid(inputs)
    return logistic * (1.0 + inputs * (1.0 - logistic))


def top_tower(picked, label_block, top_weight, score_vector):
    feats, count, width = picked.shape
    pair_dots = (
        jnp.einsum("fne,hne->nfh", picked, picked, preferred_element_type=jnp.float32)
        * width ** (-0.5)
    ).astype(jnp.bfloat16)
    pair_flat = pair_dots.reshape(count, feats * feats)
    top_pre = jnp.dot(pair_flat, top_weight, preferred_element_type=jnp.float32)
    top_hidden = jax.nn.silu(top_pre).astype(jnp.bfloat16)
    logits = jnp.dot(top_hidden, score_vector, preferred_element_type=jnp.float32)
    dlogit = loss_scale * (jax.nn.sigmoid(logits) - label_block.astype(jnp.float32))
    top_delta = (
        dlogit[:, None] * score_vector.astype(jnp.float32)[None, :] * silu_slope(top_pre)
    ).astype(jnp.bfloat16)
    pair_delta = jnp.einsum(
        "nk,jk->nj", top_delta, top_weight, preferred_element_type=jnp.float32
    ).reshape(count, feats, feats)
    pair_sym = (pair_delta + jnp.swapaxes(pair_delta, 1, 2)).astype(jnp.bfloat16)
    emb_delta = jnp.einsum(
        "nfh,hne->fne", pair_sym, picked, preferred_element_type=jnp.float32
    ) * width ** (-0.5)
    return emb_delta.astype(jnp.bfloat16)


def local(
    hash_codes, sample_index, labels, encoder_first, encoder_second, top_weight, score_vector
):
    feat_count = lax.axis_size("feat")
    encoded = (hash_codes[0].astype(jnp.float32) * (2.0 / (BUCKETS - 1)) - 1.0).astype(jnp.bfloat16)
    first_pre = jnp.dot(encoded, encoder_first[0], preferred_element_type=jnp.float32)
    first_hidden = jax.nn.silu(first_pre).astype(jnp.bfloat16)
    row_table = jnp.dot(first_hidden, encoder_second[0], preferred_element_type=jnp.float32).astype(
        jnp.bfloat16
    )
    positions = sample_index[0]
    slot_count = row_table.shape[0]
    emb_width = row_table.shape[1]
    chosen_rows = jnp.take(row_table, positions, axis=0).reshape(feat_count, -1, emb_width)
    picked = lax.all_to_all(chosen_rows, "feat", split_axis=0, concat_axis=0, tiled=True)
    emb_delta = top_tower(picked, labels[:, 0], top_weight, score_vector)
    returned = lax.all_to_all(emb_delta, "feat", split_axis=0, concat_axis=0, tiled=True)
    row_grads = jax.ops.segment_sum(
        returned.reshape(-1, emb_width).astype(jnp.float32), positions, num_segments=slot_count
    )
    row_delta = row_grads.astype(jnp.bfloat16)
    second_local = jnp.einsum(
        "rk,re->ke", first_hidden, row_delta, preferred_element_type=jnp.float32
    )
    first_back = jnp.einsum(
        "re,ke->rk", row_delta, encoder_second[0], preferred_element_type=jnp.float32
    )
    first_delta = (first_back * silu_slope(first_pre)).astype(jnp.bfloat16)
    first_local = jnp.einsum("rh,rk->hk", encoded, first_delta, preferred_element_type=jnp.float32)
    share_first, share_second = (
        lax.psum_scatter(
            first_local.astype(jnp.bfloat16), "samp", scatter_dimension=0, tiled=True
        ).astype(jnp.float32),
        lax.psum_scatter(
            second_local.astype(jnp.bfloat16), "samp", scatter_dimension=0, tiled=True
        ).astype(jnp.float32),
    )
    return (row_grads[None], share_first[None], share_second[None])


def solution(mesh):
    return jax.shard_map(
        local,
        mesh=mesh,
        in_specs=(
            P("feat", "samp", None),
            P("feat", "samp"),
            P("feat", "samp"),
            P("feat", None, None),
            P("feat", None, None),
            P(),
            P(),
        ),
        out_specs=(P("feat", "samp", None), P("feat", "samp", None), P("feat", "samp", None)),
        check_vma=False,
    )
```

profile of v0, /device:TPU:27, one launch (start us, length us, event | category | flops | bytes accessed | tf_op | source)
XLA Modules:
  0.0 204.2 jit_solution(3772232703340226694)
XLA Ops:
  7.2 0.0 copy-start
  7.2 0.8 compare_select_fusion
  8.0 0.5 broadcast.66
  8.5 1.4 reduce.3
  9.9 9.8 %multiply_convert_fusion.1 = (bf16[768,2048]{1,0:T(8,128)(2,1)S(1)}, f32[768,2048]{1,0:T(8,128)}) fusion(bf16[1,1024,2048]{2,1,0:T(8,128)(2,1)} %param.10, s32[1,768,1024]{2,1,0:T(8,128)} %param.7), kind=kOutput, calls=%fused_computation.3 | convolution fusion | flops 3232235520 | bytes 16777216 | tf_op jit(solution)/shard_map/dot_general | solution.py:46
  19.7 0.0 copy-start.5
  19.7 1.7 copy-done.5
  21.4 0.0 copy-done
  21.4 1.0 convolution_convert_fusion.2
  22.4 7.5 %gather_fusion = bf16[2048,256]{1,0:T(8,128)(2,1)S(1)} fusion(bf16[768,256]{1,0:T(8,128)(2,1)S(1)} %convolution_convert_fusion.2, s32[2048]{0:T(1024)S(1)} %broadcast_clamp_fusion), kind=kCustom, calls=%fused_computation | custom fusion | bytes 2105344 | tf_op jit(solution)/shard_map/jit(_take)/gather | solution.py:54
  29.9 0.0 copy-start.3
  29.9 0.0 copy-start.4
  29.9 1.2 broadcast_select_fusion
  31.1 0.0 copy-start.2
  31.1 4.7 %all-to-all-start = ((bf16[8,256,256]{2,1,0:T(8,128)(2,1)}), bf16[8,256,256]{2,1,0:T(8,128)(2,1)S(1)}, u32[]{:S(2)}, u32[]{:S(2)}) async-start(bf16[8,256,256]{2,1,0:T(8,128)(2,1)} %broadcast_select_fusion), calls=%async_computation | async-start | bytes 2097152 | tf_op jit(solution)/shard_map/all_to_all | solution.py:55
  35.8 0.0 reduce-scatter.5.cloned.1.call-start
  35.8 0.0 copy-done.3
  35.9 0.0 copy-done.4
  35.9 13.8 %all-to-all-done = bf16[8,256,256]{2,1,0:T(8,128)(2,1)S(1)} async-done(((bf16[8,256,256]{2,1,0:T(8,128)(2,1)}), bf16[8,256,256]{2,1,0:T(8,128)(2,1)S(1)}, u32[]{:S(2)}, u32[]{:S(2)}) %all-to-all-start) | async-done | bytes 1048608 | tf_op jit(solution)/shard_map/all_to_all | solution.py:55
  49.6 0.7 fusion.10
  50.3 0.4 copy.32
  50.7 0.0 copy-done.2
  50.7 0.3 fusion.22
  51.0 0.4 fusion.14
  51.4 0.6 convolution_bitcast_fusion
  52.0 0.4 copy.34
  52.4 1.3 copy.33
  53.8 2.0 fusion.5
  55.8 0.2 copy.36
  56.0 17.7 %all_to_all.10 = bf16[8,256,256]{2,1,0:T(8,128)(2,1)S(1)} all-to-all(bf16[8,256,256]{2,1,0:T(8,128)(2,1)S(1)} %copy.36), channel_id=1, replica_groups=mesh['feat'=8,'samp'=4] {'feat'}, dimensions={0} | all-to-all | bytes 2097152 | tf_op jit(solution)/shard_map/all_to_all | solution.py:57
  73.7 12.1 %scatter_custom_fusion = f32[768,256]{1,0:T(8,128)S(1)} fusion(s32[2048]{0:T(1024)} %bitcast.53, bf16[2048,256]{1,0:T(8,128)(2,1)S(1)} %bitcast.50, f32[]{:T(128)} %constant.9.clone.1), kind=kCustom, calls=%fused_computation.10 | custom fusion | flops 1048576 | bytes 1835520 | tf_op jit(solution)/shard_map/scatter-add | solution.py:58
  85.8 0.0 copy-start.1
  85.8 4.2 %convolution_convert_fusion.1 = bf16[2048,256]{1,0:T(8,128)(2,1)} fusion(bf16[768,2048]{1,0:T(8,128)(2,1)} %copy-done.5, f32[768,256]{1,0:T(8,128)S(1)} %scatter_custom_fusion), kind=kOutput, calls=%fused_computation.9 | convolution fusion | flops 806027264 | bytes 4980736 | tf_op jit(solution)/shard_map/rk,re->ke/dot_general | solution.py:62
  90.0 0.0 reduce-scatter.5.cloned.1.call-update
  90.0 0.0 reduce-scatter.3.cloned.1.call-start
  90.1 0.0 copy-done.1
  90.1 10.1 %convolution_convert_fusion = bf16[1024,2048]{1,0:T(8,128)(2,1)} fusion(f32[768,2048]{1,0:T(8,128)} %get-tuple-element.4, bf16[1,2048,256]{2,1,0:T(8,128)(2,1)S(1)} %copy-done, s32[1,768,1024]{2,1,0:T(8,128)} %param.7, f32[768,256]{1,0:T(8,128)S(1)} %scatter_custom_fusion), kind=kOutput, calls=%fused_computation.7 | convolution fusion | flops 4046127104 | bytes 15466496 | tf_op jit(solution)/shard_map/rh,rk->hk/dot_general | solution.py:69
  100.2 0.0 reduce-scatter.3.cloned.1.call-update
  100.3 14.4 %reduce-scatter.5.cloned.1.call-done = bf16[512,256]{1,0:T(8,128)(2,1)} async-done(((bf16[2048,256]{1,0:T(8,128)(2,1)}), bf16[512,256]{1,0:T(8,128)(2,1)}) %reduce-scatter.5.cloned.1.call-update) | async-done | bytes 262160 | tf_op jit(solution)/shard_map/reduce_scatter | solution.py:74
  114.6 1.8 bitcast_convert_fusion.1
  116.4 78.2 %reduce-scatter.3.cloned.1.call-done = bf16[256,2048]{1,0:T(8,128)(2,1)} async-done(((bf16[1024,2048]{1,0:T(8,128)(2,1)}), bf16[256,2048]{1,0:T(8,128)(2,1)}) %reduce-scatter.3.cloned.1.call-update) | async-done | bytes 1048592 | tf_op jit(solution)/shard_map/reduce_scatter | solution.py:71
  194.6 2.8 %bitcast_convert_fusion = f32[1,256,2048]{2,1,0:T(8,128)} fusion(bf16[256,2048]{1,0:T(8,128)(2,1)} %reduce-scatter.3.cloned.1.call-done), kind=kLoop, calls=%fused_computation.17 | loop fusion | flops 524288 | bytes 3145728 | tf_op jit(solution)/shard_map/broadcast_in_dim | solution.py:78
  (7 shorter events, 0.0 us)
Async XLA Ops:
  7.2 14.2 %copy-start = (bf16[1,2048,256]{2,1,0:T(8,128)(2,1)S(1)}, bf16[1,2048,256]{2,1,0:T(8,128)(2,1)}, u32[]{:S(2)}) copy-start(bf16[1,2048,256]{2,1,0:T(8,128)(2,1)} %param.11) | copy-start | bytes 3145732
  19.7 1.7 copy-start.5
  29.9 6.0 %copy-start.3 = (bf16[1024]{0:T(1024)(128)(2,1)S(1)}, bf16[1024]{0:T(1024)(128)(2,1)}, u32[]{:S(2)}) copy-start(bf16[1024]{0:T(1024)(128)(2,1)} %param.13) | copy-start | bytes 6148
  29.9 6.0 %copy-start.4 = (s32[256,1]{0,1:T(1,128)S(1)}, s32[256,1]{0,1:T(1,128)}, u32[]{:S(2)}) copy-start(s32[256,1]{0,1:T(1,128)} %param.9) | copy-start | bytes 3076
  31.1 19.6 %copy-start.2 = (bf16[64,1024]{1,0:T(8,128)(2,1)S(1)}, bf16[64,1024]{1,0:T(8,128)(2,1)}, u32[]{:S(2)}) copy-start(bf16[64,1024]{1,0:T(8,128)(2,1)} %param.12) | copy-start | bytes 393220
  31.1 18.5 %all-to-all-start = ((bf16[8,256,256]{2,1,0:T(8,128)(2,1)}), bf16[8,256,256]{2,1,0:T(8,128)(2,1)S(1)}, u32[]{:S(2)}, u32[]{:S(2)}) async-start(bf16[8,256,256]{2,1,0:T(8,128)(2,1)} %broadcast_select_fusion), calls=%async_computation | async-start | bytes 2097152 | tf_op jit(solution)/shard_map/all_to_all | solution.py:55
  35.8 78.8 %reduce-scatter.5.cloned.1.call-start = ((), (), s32[]{:S(2)}) async-start(), calls=%async_computation.5 | async-start | bytes 1310720 | tf_op jit(solution)/shard_map/reduce_scatter | solution.py:74
  85.8 4.3 %copy-start.1 = (f32[768,256]{1,0:T(8,128)}, f32[768,256]{1,0:T(8,128)S(1)}, u32[]{:S(2)}) copy-start(f32[768,256]{1,0:T(8,128)S(1)} %scatter_custom_fusion) | copy-start | bytes 2359300
  90.0 104.6 %reduce-scatter.3.cloned.1.call-start = ((), (), s32[]{:S(2)}) async-start(), calls=%async_computation.4 | async-start | bytes 5242880 | tf_op jit(solution)/shard_map/reduce_scatter | solution.py:71
Sparse Core Ops, SparseCore 0:
  90.2 24.4 reduce-scatter.4
  117.0 77.5 reduce-scatter.2
where the time goes:
time: 207 us; the launch traced here: 204 us
  waiting for transfers between devices  106 us (51%)
  matrix products  29.1 us (14%)
  other arithmetic  20.1 us (10%)
  blocking collectives  17.7 us (9%)
  between operations  14.2 us (7%)
  local copies, waits for them, and re-layouts  12.1 us (6%)
  starting transfers between devices  4.74 us (2%)
    reduce_scatter x1, waiting for transfers between devices, local(): lax.psum_scatter(first_local.astype(jnp.bfloat16), 'samp', scatter_dimens...  78.2 us
    all_to_all x1, blocking collectives, local(): lax.all_to_all(emb_delta, 'feat', split_axis=0, concat_axis=0, tiled=True)  17.7 us
    reduce_scatter x1, waiting for transfers between devices, local(): lax.psum_scatter(second_local.astype(jnp.bfloat16), 'samp', scatter_dimen...  14.4 us
    all_to_all x1, waiting for transfers between devices, local(): lax.all_to_all(chosen_rows, 'feat', split_axis=0, concat_axis=0, tiled=True)  13.8 us
    scatter-add x1, other arithmetic, local(): jax.ops.segment_sum(returned.reshape(-1, emb_width).astype(jnp.float32),...  12.1 us
    dot_general x1, matrix products, local(): jnp.einsum('rh,rk->hk', encoded, first_delta, preferred_element_type=jnp....  10.1 us
    dot_general x1, matrix products, local(): jnp.dot(encoded, encoder_first[0], preferred_element_type=jnp.float32)  9.76 us
    gather x1, local copies, waits for them, and re-layouts, local(): jnp.take(row_table, positions, axis=0).reshape(feat_count, -1, emb_width)  7.5 us
  transfers between devices with their start and end apart: 3, of which 3 were waited for; matrix products, arithmetic and copies ran while one was open for 6% of the time, Pallas kernels for 0%

commit v1 on v0

--- a/solution.py
+++ b/solution.py
@@ -42,38 +42,56 @@
     hash_codes, sample_index, labels, encoder_first, encoder_second, top_weight, score_vector
 ):
     feat_count = lax.axis_size("feat")
+    samp_count = lax.axis_size("samp")
+    samp_at = lax.axis_index("samp")
+    weight_first, weight_second = encoder_first[0], encoder_second[0]
+    hash_count, hidden_count = weight_first.shape
+    emb_width = weight_second.shape[1]
     encoded = (hash_codes[0].astype(jnp.float32) * (2.0 / (BUCKETS - 1)) - 1.0).astype(jnp.bfloat16)
-    first_pre = jnp.dot(encoded, encoder_first[0], preferred_element_type=jnp.float32)
+    slot_count = encoded.shape[0]
+    encoded_all = lax.all_gather(encoded, "samp", axis=0, tiled=True)
+    first_pre = jnp.dot(encoded, weight_first, preferred_element_type=jnp.float32)
     first_hidden = jax.nn.silu(first_pre).astype(jnp.bfloat16)
-    row_table = jnp.dot(first_hidden, encoder_second[0], preferred_element_type=jnp.float32).astype(
+    row_table = jnp.dot(first_hidden, weight_second, preferred_element_type=jnp.float32).astype(
         jnp.bfloat16
     )
     positions = sample_index[0]
-    slot_count = row_table.shape[0]
-    emb_width = row_table.shape[1]
-    chosen_rows = jnp.take(row_table, positions, axis=0).reshape(feat_count, -1, emb_width)
+    slots = lax.broadcasted_iota(jnp.int32, (positions.shape[0], slot_count), 1)
+    chooser = (positions[:, None] == slots).astype(jnp.bfloat16)
+    chosen_rows = (
+        jnp.dot(chooser, row_table, preferred_element_type=jnp.float32)
+        .astype(jnp.bfloat16)
+        .reshape(feat_count, -1, emb_width)
+    )
     picked = lax.all_to_all(chosen_rows, "feat", split_axis=0, concat_axis=0, tiled=True)
     emb_delta = top_tower(picked, labels[:, 0], top_weight, score_vector)
     returned = lax.all_to_all(emb_delta, "feat", split_axis=0, concat_axis=0, tiled=True)
-    row_grads = jax.ops.segment_sum(
-        returned.reshape(-1, emb_width).astype(jnp.float32), positions, num_segments=slot_count
+    slots_back = lax.broadcasted_iota(jnp.int32, (slot_count, positions.shape[0]), 0)
+    placer = (positions[None, :] == slots_back).astype(jnp.bfloat16)
+    row_grads = jnp.dot(
+        placer, returned.reshape(-1, emb_width), preferred_element_type=jnp.float32
     )
-    row_delta = row_grads.astype(jnp.bfloat16)
-    second_local = jnp.einsum(
-        "rk,re->ke", first_hidden, row_delta, preferred_element_type=jnp.float32
+    row_delta_all = lax.all_gather(row_grads.astype(jnp.bfloat16), "samp", axis=0, tiled=True)
+
+    slope_all = silu_slope(
+        jnp.dot(encoded_all, weight_first, preferred_element_type=jnp.float32)
+    ).astype(jnp.bfloat16)
+    share = hidden_count // samp_count
+    weight_share = lax.dynamic_slice_in_dim(weight_first, samp_at * share, share, axis=1)
+    hidden_share = jax.nn.silu(
+        jnp.dot(encoded_all, weight_share, preferred_element_type=jnp.float32)
+    ).astype(jnp.bfloat16)
+    depth = hash_count // samp_count
+    encoded_share = lax.dynamic_slice_in_dim(encoded_all, samp_at * depth, depth, axis=1)
+    share_second = jnp.einsum(
+        "rk,re->ke", hidden_share, row_delta_all, preferred_element_type=jnp.float32
     )
     first_back = jnp.einsum(
-        "re,ke->rk", row_delta, encoder_second[0], preferred_element_type=jnp.float32
+        "re,ke->rk", row_delta_all, weight_second, preferred_element_type=jnp.float32
     )
-    first_delta = (first_back * silu_slope(first_pre)).astype(jnp.bfloat16)
-    first_local = jnp.einsum("rh,rk->hk", encoded, first_delta, preferred_element_type=jnp.float32)
-    share_first, share_second = (
-        lax.psum_scatter(
-            first_local.astype(jnp.bfloat16), "samp", scatter_dimension=0, tiled=True
-        ).astype(jnp.float32),
-        lax.psum_scatter(
-            second_local.astype(jnp.bfloat16), "samp", scatter_dimension=0, tiled=True
-        ).astype(jnp.float32),
+    first_delta = (first_back * slope_all.astype(jnp.float32)).astype(jnp.bfloat16)
+    share_first = jnp.einsum(
+        "rh,rk->hk", encoded_share, first_delta, preferred_element_type=jnp.float32
     )
     return (row_grads[None], share_first[None], share_second[None])
 

time: 207 us -> 201 us (0.971)
  matrix products: 29.1 us -> 62.4 us
  blocking collectives: 17.7 us -> 0 us
  other arithmetic: 20.1 us -> 3.6 us
  local copies, waits for them, and re-layouts: 12.1 us -> 3.33 us
  starting transfers between devices: 4.74 us -> 9.7 us
    reduce_scatter x2 -> x0, waiting for transfers between devices: 92.6 us -> none  [the longest x1 78.2 us: local(): lax.psum_scatter(first_local.astype(jnp.bfloat16), 'samp', scatter_dimens...]
    all_gather x0 -> x2, waiting for transfers between devices: none -> 76.1 us  [the longest x1 57.5 us: local(): encoded_all = lax.all_gather(encoded, 'samp', axis=0, tiled=True)]
    dot_general x4 -> x6, matrix products: 25.1 us -> 58.4 us  [the longest x1 19.6 us: local(): jnp.dot(encoded_all, weight_first, preferred_element_type=jnp.float32)]
    all_to_all x1 -> x0, blocking collectives: 17.7 us -> none  [local(): lax.all_to_all(emb_delta, 'feat', split_axis=0, concat_axis=0, tiled=True)]
    all_to_all x0 -> x1, waiting for transfers between devices: none -> 13.9 us  [local(): lax.all_to_all(emb_delta, 'feat', split_axis=0, concat_axis=0, tiled=True)]
    scatter-add x1 -> x0, other arithmetic: 12.1 us -> none  [local(): jax.ops.segment_sum(returned.reshape(-1, emb_width).astype(jnp.float32),...]
    gather x1 -> x0, local copies, waits for them, and re-layouts: 7.5 us -> none  [local(): jnp.take(row_table, positions, axis=0).reshape(feat_count, -1, emb_width)]
    all_to_all x0 -> x1, starting transfers between devices: none -> 4.96 us  [local(): lax.all_to_all(emb_delta, 'feat', split_axis=0, concat_axis=0, tiled=True)]
  transfers between devices with their start and end apart: 3 -> 4, of which waited for: 3 -> 4; matrix products, arithmetic and copies ran while one was open for 6% -> 19% of each run, Pallas kernels for 0% -> 0%
where the time goes in v1:
time: 201 us; the launch traced here: 197 us
  waiting for transfers between devices  104 us (52%)
  matrix products  62.4 us (31%)
  between operations  14.1 us (7%)
  starting transfers between devices  9.7 us (5%)
  other arithmetic  3.6 us (2%)
  local copies, waits for them, and re-layouts  3.33 us (2%)
    all_gather x1, waiting for transfers between devices, local(): encoded_all = lax.all_gather(encoded, 'samp', axis=0, tiled=True)  57.5 us
    dot_general x1, matrix products, local(): jnp.dot(encoded_all, weight_first, preferred_element_type=jnp.float32)  19.6 us
    all_gather x1, waiting for transfers between devices, local(): lax.all_gather(row_grads.astype(jnp.bfloat16), 'samp', axis=0, tiled=True)  18.6 us
    dot_general x1, matrix products, local(): jnp.einsum('rh,rk->hk', encoded_share, first_delta, preferred_element_typ...  17.7 us
    all_to_all x1, waiting for transfers between devices, local(): lax.all_to_all(emb_delta, 'feat', split_axis=0, concat_axis=0, tiled=True)  13.9 us
    all_to_all x1, waiting for transfers between devices, local(): lax.all_to_all(chosen_rows, 'feat', split_axis=0, concat_axis=0, tiled=True)  13.9 us
    dot_general x1, matrix products, local(): jnp.einsum('rk,re->ke', hidden_share, row_delta_all, preferred_element_ty...  9.72 us
    dot_general x1, matrix products, local(): jnp.dot(first_hidden, weight_second, preferred_element_type=jnp.float32)  7.05 us
  transfers between devices with their start and end apart: 4, of which 4 were waited for; matrix products, arithmetic and copies ran while one was open for 19% of the time, Pallas kernels for 0%

profile of v1, /device:TPU:27, one launch (start us, length us, event | category | flops | bytes accessed | tf_op | source)
XLA Modules:
  0.0 197.1 jit_solution(6953485504392931628)
XLA Ops:
  7.2 0.0 copy-start
  7.2 0.0 all-gather.6.cloned.1.call-start
  7.2 3.6 %add_convert_fusion = bf16[1,768,1024]{2,1,0:T(8,128)(2,1)} fusion(s32[1,768,1024]{2,1,0:T(8,128)} %param.7), kind=kLoop, calls=%fused_computation.17 | loop fusion | flops 3145728 | bytes 4718592 | tf_op jit(solution)/shard_map/convert_element_type | solution.py:50
  10.8 0.0 all-gather.6.cloned.1.call-update
  10.8 0.0 copy-done
  10.8 0.0 copy-start.5
  10.9 7.0 %fusion.31 = bf16[768,256]{1,0:T(8,128)(2,1)S(1)} fusion(bf16[1,1024,2048]{2,1,0:T(8,128)(2,1)} %param.10, bf16[1,768,1024]{2,1,0:T(8,128)(2,1)} %add_convert_fusion, bf16[1,2048,256]{2,1,0:T(8,128)(2,1)S(1)} %copy-done), kind=kOutput, calls=%fused_computation.29 | convolution fusion | flops 4034592768 | bytes 7208960 | tf_op jit(solution)/shard_map/dot_general | solution.py:55
  17.9 0.0 copy-start.2
  17.9 0.0 copy-start.3
  17.9 0.0 copy-done.5
  17.9 2.3 %fusion.17 = bf16[2048,256]{1,0:T(8,128)(2,1)} fusion(bf16[768,256]{1,0:T(8,128)(2,1)S(1)} %fusion.31, s32[2048]{0:T(1024)S(1)} %bitcast.73), kind=kOutput, calls=%fused_computation.23 | convolution fusion | flops 807403520 | bytes 1449984 | tf_op jit(solution)/shard_map/dot_general | solution.py:62
  20.2 0.0 copy-start.1
  20.2 4.7 %all-to-all-start = ((bf16[8,256,256]{2,1,0:T(8,128)(2,1)}), bf16[8,256,256]{2,1,0:T(8,128)(2,1)S(1)}, u32[]{:S(2)}, u32[]{:S(2)}) async-start(bf16[8,256,256]{2,1,0:T(8,128)(2,1)} %bitcast.4), calls=%async_computation | async-start | bytes 2097152 | tf_op jit(solution)/shard_map/all_to_all | solution.py:66
  24.9 0.0 copy-done.2
  24.9 0.0 copy-done.3
  25.0 13.9 %all-to-all-done = bf16[8,256,256]{2,1,0:T(8,128)(2,1)S(1)} async-done(((bf16[8,256,256]{2,1,0:T(8,128)(2,1)}), bf16[8,256,256]{2,1,0:T(8,128)(2,1)S(1)}, u32[]{:S(2)}, u32[]{:S(2)}) %all-to-all-start) | async-done | bytes 1048608 | tf_op jit(solution)/shard_map/all_to_all | solution.py:66
  38.8 0.7 fusion.47
  39.5 0.4 copy.27
  39.9 0.0 copy-done.1
  39.9 0.3 fusion.53
  40.2 0.4 fusion.51
  40.6 0.6 convolution_bitcast_fusion
  41.2 0.4 copy.29
  41.6 1.3 copy.28
  43.0 2.0 %fusion.30 = bf16[8,256,256]{2,0,1:T(8,128)(2,1)S(1)} fusion(bf16[8,256,256]{2,1,0:T(8,128)(2,1)S(1)} %all-to-all-done, f32[256,8,8]{2,1,0:T(8,128)S(1)} %copy.29, f32[256,8,8]{1,2,0:T(8,128)} %copy.28), kind=kOutput, calls=%fused_computation.28 | convolution fusion | flops 9469952 | bytes 2228224 | tf_op jit(solution)/shard_map/nfh,hne->fne/dot_general | solution.py:35
  45.0 1.2 copy.31
  46.2 5.0 %all-to-all-start.1 = ((bf16[8,256,256]{2,1,0:T(8,128)(2,1)}), bf16[8,256,256]{2,1,0:T(8,128)(2,1)S(1)}, u32[]{:S(2)}, u32[]{:S(2)}) async-start(bf16[8,256,256]{2,1,0:T(8,128)(2,1)} %copy.31), calls=%async_computation.1 | async-start | bytes 2097152 | tf_op jit(solution)/shard_map/all_to_all | solution.py:68
  51.1 0.0 all-gather.4.cloned.1.call-start
  51.1 13.9 %all-to-all-done.1 = bf16[8,256,256]{2,1,0:T(8,128)(2,1)S(1)} async-done(((bf16[8,256,256]{2,1,0:T(8,128)(2,1)}), bf16[8,256,256]{2,1,0:T(8,128)(2,1)S(1)}, u32[]{:S(2)}, u32[]{:S(2)}) %all-to-all-start.1) | async-done | bytes 1048608 | tf_op jit(solution)/shard_map/all_to_all | solution.py:68
  65.1 2.1 %fusion.66 = (bf16[768,256]{1,0:T(8,128)(2,1)}, f32[768,256]{1,0:T(8,128)}) fusion(bf16[2048,256]{1,0:T(8,128)(2,1)S(1)} %bitcast.70, s32[2048]{0:T(1024)S(1)} %bitcast.74), kind=kOutput, calls=%fused_computation.59 | convolution fusion | flops 807075840 | bytes 2236416 | tf_op jit(solution)/shard_map/dot_general | solution.py:71
  67.2 0.0 all-gather.4.cloned.1.call-update
  67.2 57.5 %all-gather.6.cloned.1.call-done = bf16[1,3072,1024]{2,1,0:T(8,128)(2,1)} async-done(((bf16[1,768,1024]{2,1,0:T(8,128)(2,1)}), bf16[1,3072,1024]{2,1,0:T(8,128)(2,1)}) %all-gather.6.cloned.1.call-update) | async-done | bytes 6291472 | tf_op jit(solution)/shard_map/all_gather | solution.py:52
  124.7 19.6 %fusion.3 = f32[3072,2048]{1,0:T(8,128)} fusion(bf16[1,3072,1024]{2,1,0:T(8,128)(2,1)} %all-gather.6.cloned.1.call-done, bf16[1,1024,2048]{2,1,0:T(8,128)(2,1)} %param.10), kind=kOutput, calls=%fused_computation.4 | convolution fusion | flops 12884901888 | bytes 35651584 | tf_op jit(solution)/shard_map/dot_general | solution.py:77
  144.3 18.6 %all-gather.4.cloned.1.call-done = bf16[3072,256]{1,0:T(8,128)(2,1)} async-done(((bf16[768,256]{1,0:T(8,128)(2,1)}), bf16[3072,256]{1,0:T(8,128)(2,1)}) %all-gather.4.cloned.1.call-update) | async-done | bytes 1572880 | tf_op jit(solution)/shard_map/all_gather | solution.py:74
  162.9 0.0 copy-start.4
  162.9 9.7 %fusion.36 = f32[1,512,256]{2,1,0:T(8,128)} fusion(bf16[3072,256]{1,0:T(8,128)(2,1)} %all-gather.4.cloned.1.call-done, bf16[1,3072,1024]{2,1,0:T(8,128)(2,1)} %all-gather.6.cloned.1.call-done, bf16[1,1024,2048]{2,1,0:T(8,128)(2,1)} %param.10, s32[]{:T(128)S(6)} %select_n.7), kind=kOutput, calls=%fused_computation.30 | convolution fusion | flops 4034396160 | bytes 9437188 | tf_op jit(solution)/shard_map/rk,re->ke/dot_general | solution.py:86
  172.6 0.0 copy-done.4
  172.6 17.7 %fusion.16 = f32[1,256,2048]{2,1,0:T(8,128)} fusion(f32[3072,2048]{1,0:T(8,128)} %fusion.3, bf16[3072,256]{1,0:T(8,128)(2,1)S(1)} %copy-done.4, bf16[1,3072,1024]{2,1,0:T(8,128)(2,1)} %all-gather.6.cloned.1.call-done, s32[]{:T(128)S(6)} %select_n.6, bf16[1,2048,256]{2,1,0:T(8,128)(2,1)S(1)} %copy-done), kind=kOutput, calls=%fused_computation.22 | convolution fusion | flops 6511656960 | bytes 31457284 | tf_op jit(solution)/shard_map/rh,rk->hk/dot_general | solution.py:93
  (4 shorter events, 0.0 us)
Async XLA Ops:
  7.2 3.7 %copy-start = (bf16[1,2048,256]{2,1,0:T(8,128)(2,1)S(1)}, bf16[1,2048,256]{2,1,0:T(8,128)(2,1)}, u32[]{:S(2)}) copy-start(bf16[1,2048,256]{2,1,0:T(8,128)(2,1)} %param.11) | copy-start | bytes 3145732
  7.2 117.5 %all-gather.6.cloned.1.call-start = ((), (), s32[]{:S(2)}) async-start(), calls=%async_computation.3 | async-start | bytes 7864320 | tf_op jit(solution)/shard_map/all_gather | solution.py:52
  10.8 7.1 %copy-start.5 = (s32[1,2048]{1,0:T(1,128)S(1)}, s32[1,2048]{1,0:T(1,128)}, u32[]{:S(2)}) copy-start(s32[1,2048]{1,0:T(1,128)} %param.8) | copy-start | bytes 24580
  17.9 7.0 %copy-start.2 = (bf16[1024]{0:T(1024)(128)(2,1)S(1)}, bf16[1024]{0:T(1024)(128)(2,1)}, u32[]{:S(2)}) copy-start(bf16[1024]{0:T(1024)(128)(2,1)} %param.13) | copy-start | bytes 6148
  17.9 7.0 %copy-start.3 = (s32[256,1]{0,1:T(1,128)S(1)}, s32[256,1]{0,1:T(1,128)}, u32[]{:S(2)}) copy-start(s32[256,1]{0,1:T(1,128)} %param.9) | copy-start | bytes 3076
  20.2 19.7 %copy-start.1 = (bf16[64,1024]{1,0:T(8,128)(2,1)S(1)}, bf16[64,1024]{1,0:T(8,128)(2,1)}, u32[]{:S(2)}) copy-start(bf16[64,1024]{1,0:T(8,128)(2,1)} %param.12) | copy-start | bytes 393220
  20.2 18.6 %all-to-all-start = ((bf16[8,256,256]{2,1,0:T(8,128)(2,1)}), bf16[8,256,256]{2,1,0:T(8,128)(2,1)S(1)}, u32[]{:S(2)}, u32[]{:S(2)}) async-start(bf16[8,256,256]{2,1,0:T(8,128)(2,1)} %bitcast.4), calls=%async_computation | async-start | bytes 2097152 | tf_op jit(solution)/shard_map/all_to_all | solution.py:66
  46.2 18.9 %all-to-all-start.1 = ((bf16[8,256,256]{2,1,0:T(8,128)(2,1)}), bf16[8,256,256]{2,1,0:T(8,128)(2,1)S(1)}, u32[]{:S(2)}, u32[]{:S(2)}) async-start(bf16[8,256,256]{2,1,0:T(8,128)(2,1)} %copy.31), calls=%async_computation.1 | async-start | bytes 2097152 | tf_op jit(solution)/shard_map/all_to_all | solution.py:68
  51.1 111.8 %all-gather.4.cloned.1.call-start = ((), (), s32[]{:S(2)}) async-start(), calls=%async_computation.2 | async-start | bytes 1966080 | tf_op jit(solution)/shard_map/all_gather | solution.py:74
  162.9 9.7 %copy-start.4 = (bf16[3072,256]{1,0:T(8,128)(2,1)S(1)}, bf16[3072,256]{1,0:T(8,128)(2,1)}, u32[]{:S(2)}) copy-start(bf16[3072,256]{1,0:T(8,128)(2,1)} %all-gather.4.cloned.1.call-done) | copy-start | bytes 4718596
Sparse Core Ops, SparseCore 0:
  11.0 113.7 all-gather.5
  126.9 35.9 all-gather.3

commit v2 on v1

--- a/solution.py
+++ b/solution.py
@@ -44,14 +44,18 @@
     feat_count = lax.axis_size("feat")
     samp_count = lax.axis_size("samp")
     samp_at = lax.axis_index("samp")
+    half = samp_count // 2
+    across = [(i, i // 2 * 2 + (i + 1) % 2) for i in range(samp_count)]
     weight_first, weight_second = encoder_first[0], encoder_second[0]
     hash_count, hidden_count = weight_first.shape
     emb_width = weight_second.shape[1]
     encoded = (hash_codes[0].astype(jnp.float32) * (2.0 / (BUCKETS - 1)) - 1.0).astype(jnp.bfloat16)
     slot_count = encoded.shape[0]
-    encoded_all = lax.all_gather(encoded, "samp", axis=0, tiled=True)
+    encoded = lax.optimization_barrier(encoded)
+    encoded_far = lax.ppermute(encoded, "samp", across)
     first_pre = jnp.dot(encoded, weight_first, preferred_element_type=jnp.float32)
     first_hidden = jax.nn.silu(first_pre).astype(jnp.bfloat16)
+    slope = silu_slope(first_pre).astype(jnp.bfloat16)
     row_table = jnp.dot(first_hidden, weight_second, preferred_element_type=jnp.float32).astype(
         jnp.bfloat16
     )
@@ -65,34 +69,55 @@
     )
     picked = lax.all_to_all(chosen_rows, "feat", split_axis=0, concat_axis=0, tiled=True)
     emb_delta = top_tower(picked, labels[:, 0], top_weight, score_vector)
+    emb_delta, slope, first_hidden = lax.optimization_barrier((emb_delta, slope, first_hidden))
     returned = lax.all_to_all(emb_delta, "feat", split_axis=0, concat_axis=0, tiled=True)
     slots_back = lax.broadcasted_iota(jnp.int32, (slot_count, positions.shape[0]), 0)
     placer = (positions[None, :] == slots_back).astype(jnp.bfloat16)
     row_grads = jnp.dot(
         placer, returned.reshape(-1, emb_width), preferred_element_type=jnp.float32
     )
-    row_delta_all = lax.all_gather(row_grads.astype(jnp.bfloat16), "samp", axis=0, tiled=True)
+    row_delta = row_grads.astype(jnp.bfloat16)
+    row_delta_far = lax.ppermute(row_delta, "samp", across)
 
-    slope_all = silu_slope(
-        jnp.dot(encoded_all, weight_first, preferred_element_type=jnp.float32)
-    ).astype(jnp.bfloat16)
+    first_pre_far = jnp.dot(encoded_far, weight_first, preferred_element_type=jnp.float32)
+    hidden_far, slope_far = lax.optimization_barrier(
+        (
+            jax.nn.silu(first_pre_far).astype(jnp.bfloat16),
+            silu_slope(first_pre_far).astype(jnp.bfloat16),
+        )
+    )
+
+    def delta_of(rows, factor):
+        back = jnp.einsum("re,ke->rk", rows, weight_second, preferred_element_type=jnp.float32)
+        return (back * factor.astype(jnp.float32)).astype(jnp.bfloat16)
+
+    near = (encoded, first_hidden, row_delta, delta_of(row_delta, slope))
+    far = (encoded_far, hidden_far, row_delta_far, delta_of(row_delta_far, slope_far))
+    depth = hash_count // samp_count
     share = hidden_count // samp_count
-    weight_share = lax.dynamic_slice_in_dim(weight_first, samp_at * share, share, axis=1)
-    hidden_share = jax.nn.silu(
-        jnp.dot(encoded_all, weight_share, preferred_element_type=jnp.float32)
-    ).astype(jnp.bfloat16)
-    depth = hash_count // samp_count
-    encoded_share = lax.dynamic_slice_in_dim(encoded_all, samp_at * depth, depth, axis=1)
-    share_second = jnp.einsum(
-        "rk,re->ke", hidden_share, row_delta_all, preferred_element_type=jnp.float32
-    )
-    first_back = jnp.einsum(
-        "re,ke->rk", row_delta_all, weight_second, preferred_element_type=jnp.float32
-    )
-    first_delta = (first_back * slope_all.astype(jnp.float32)).astype(jnp.bfloat16)
-    share_first = jnp.einsum(
-        "rh,rk->hk", encoded_share, first_delta, preferred_element_type=jnp.float32
-    )
+
+    def first_part(group, at):
+        columns = lax.dynamic_slice_in_dim(group[0], at * depth, depth, axis=1)
+        return jnp.einsum("rh,rk->hk", columns, group[3], preferred_element_type=jnp.float32)
+
+    def second_part(group, at):
+        columns = lax.dynamic_slice_in_dim(group[1], at * share, share, axis=1)
+        return jnp.einsum("rk,re->ke", columns, group[2], preferred_element_type=jnp.float32)
+
+    firsts, seconds = [], []
+    for step in range(1, half):
+        target = (samp_at + 2 * step) % samp_count
+        pairs = [(i, (i + 2 * step) % samp_count) for i in range(samp_count)]
+        first_out = (first_part(near, target) + first_part(far, target)).astype(jnp.bfloat16)
+        firsts.append(lax.ppermute(first_out, "samp", pairs))
+        second_out = (second_part(near, target) + second_part(far, target)).astype(jnp.bfloat16)
+        seconds.append(lax.ppermute(second_out, "samp", pairs))
+    share_first = first_part(near, samp_at) + first_part(far, samp_at)
+    share_second = second_part(near, samp_at) + second_part(far, samp_at)
+    for arrived in firsts:
+        share_first = share_first + arrived.astype(jnp.float32)
+    for arrived in seconds:
+        share_second = share_second + arrived.astype(jnp.float32)
     return (row_grads[None], share_first[None], share_second[None])
 
 

time: 201 us -> 149 us (0.74)
  matrix products: 62.4 us -> 41.8 us
  waiting for transfers between devices: 104 us -> 84.7 us
  between operations: 14.1 us -> 0.81 us
  starting transfers between devices: 9.7 us -> 12.5 us
    all_gather x2 -> x0, waiting for transfers between devices: 76.1 us -> none  [the longest x1 57.5 us: local(): encoded_all = lax.all_gather(encoded, 'samp', axis=0, tiled=True)]
    ppermute x0 -> x4, waiting for transfers between devices: none -> 71 us  [the longest x1 55.3 us: local(): seconds.append(lax.ppermute(second_out, 'samp', pairs))]
    dot_general x4 -> x12, matrix products: 54 us -> 29.5 us  [the longest x1 10.4 us: local(): jnp.dot(encoded_far, weight_first, preferred_element_type=jnp.float32)]
    all_to_all x1, waiting for transfers between devices: 13.9 us -> 0.01 us  [local(): lax.all_to_all(emb_delta, 'feat', split_axis=0, concat_axis=0, tiled=True)]
    dot_general x1, matrix products: 2.27 us -> 6.24 us  [local(): jnp.dot(chooser, row_table, preferred_element_type=jnp.float32)]
    ppermute x0 -> x4, starting transfers between devices: none -> 2.83 us  [the longest x1 2.38 us: local(): seconds.append(lax.ppermute(second_out, 'samp', pairs))]
  transfers between devices with their start and end apart: 4 -> 6, of which waited for: 4 -> 4; matrix products, arithmetic and copies ran while one was open for 19% -> 16% of each run, Pallas kernels for 0% -> 0%
where the time goes in v2:
time: 149 us; the launch traced here: 147 us
  waiting for transfers between devices  84.7 us (57%)
  matrix products  41.8 us (28%)
  starting transfers between devices  12.5 us (8%)
  local copies, waits for them, and re-layouts  4.76 us (3%)
  other arithmetic  2.53 us (2%)
    ppermute x1, waiting for transfers between devices, local(): seconds.append(lax.ppermute(second_out, 'samp', pairs))  55.3 us
    all_to_all x1, waiting for transfers between devices, local(): lax.all_to_all(chosen_rows, 'feat', split_axis=0, concat_axis=0, tiled=True)  13.7 us
    dot_general x1, matrix products, local(): jnp.dot(encoded_far, weight_first, preferred_element_type=jnp.float32)  10.4 us
    ppermute x1, waiting for transfers between devices, local(): encoded_far = lax.ppermute(encoded, 'samp', across)  9.68 us
    dot_general x4, matrix products, first_part(): jnp.einsum('rh,rk->hk', columns, group[3], preferred_element_type=jnp.flo...  7.56 us
    dot_general x1, matrix products, local(): jnp.dot(encoded, weight_first, preferred_element_type=jnp.float32)  7.02 us
    dot_general x1, matrix products, local(): jnp.dot(chooser, row_table, preferred_element_type=jnp.float32)  6.24 us
    ppermute x1, waiting for transfers between devices, local(): row_delta_far = lax.ppermute(row_delta, 'samp', across)  6.05 us
  transfers between devices with their start and end apart: 6, of which 4 were waited for; matrix products, arithmetic and copies ran while one was open for 16% of the time, Pallas kernels for 0%

profile of v2, /device:TPU:27, one launch (start us, length us, event | category | flops | bytes accessed | tf_op | source)
XLA Modules:
  0.0 147.0 jit_solution(15510484497139298394)
XLA Ops:
  0.6 0.0 copy-start
  0.6 0.0 copy-start.9
  0.7 2.5 %fusion.12 = bf16[768,1024]{1,0:T(8,128)(2,1)S(1)} fusion(s32[1,768,1024]{2,1,0:T(8,128)} %param.7), kind=kLoop, calls=%fused_computation.26 | loop fusion | flops 3145728 | bytes 4718592 | tf_op jit(solution)/shard_map/convert_element_type | solution.py:52
  3.2 0.7 copy-done.9
  3.9 0.0 copy-start.1
  3.9 0.0 copy-start.10
  3.9 7.0 %multiply_convert_fusion.4 = (bf16[768,2048]{1,0:T(8,128)(2,1)}, bf16[768,2048]{1,0:T(8,128)(2,1)}) fusion(bf16[768,1024]{1,0:T(8,128)(2,1)S(1)} %fusion.12, bf16[1,1024,2048]{2,1,0:T(8,128)(2,1)S(1)} %copy-done.9), kind=kOutput, calls=%fused_computation.5 | convolution fusion | flops 3236954112 | bytes 12058624 | tf_op jit(solution)/shard_map/dot_general | solution.py:56
  10.9 0.0 copy-done.1
  10.9 0.0 copy-done
  10.9 0.0 copy-done.10
  10.9 0.0 copy-start.7
  10.9 0.0 copy-start.8
  10.9 6.2 %fusion.11 = bf16[2048,256]{1,0:T(8,128)(2,1)} fusion(s32[2048]{0:T(1024)S(1)} %bitcast.62, bf16[768,2048]{1,0:T(8,128)(2,1)} %get-tuple-element.11, bf16[1,2048,256]{2,1,0:T(8,128)(2,1)S(1)} %copy-done), kind=kOutput, calls=%fused_computation.24 | convolution fusion | flops 1612906496 | bytes 5251072 | tf_op jit(solution)/shard_map/dot_general | solution.py:66
  17.2 0.0 copy-start.6
  17.2 4.7 %all-to-all-start = ((bf16[8,256,256]{2,1,0:T(8,128)(2,1)}), bf16[8,256,256]{2,1,0:T(8,128)(2,1)S(1)}, u32[]{:S(2)}, u32[]{:S(2)}) async-start(bf16[8,256,256]{2,1,0:T(8,128)(2,1)} %bitcast.4), calls=%async_computation | async-start | bytes 2097152 | tf_op jit(solution)/shard_map/all_to_all | solution.py:70
  21.9 0.2 collective-permute-start
  22.0 0.0 copy-done.7
  22.1 0.0 copy-done.8
  22.1 13.7 %all-to-all-done = bf16[8,256,256]{2,1,0:T(8,128)(2,1)S(1)} async-done(((bf16[8,256,256]{2,1,0:T(8,128)(2,1)}), bf16[8,256,256]{2,1,0:T(8,128)(2,1)S(1)}, u32[]{:S(2)}, u32[]{:S(2)}) %all-to-all-start) | async-done | bytes 1048608 | tf_op jit(solution)/shard_map/all_to_all | solution.py:70
  35.8 0.7 fusion.21
  36.5 0.4 copy.27
  36.9 0.0 copy-done.6
  36.9 0.3 fusion.41
  37.2 0.4 fusion.33
  37.6 0.6 convolution_bitcast_fusion
  38.2 0.4 copy.28
  38.6 1.3 copy.29
  39.9 2.1 %fusion.13 = bf16[8,256,256]{2,0,1:T(8,128)(2,1)S(1)} fusion(bf16[8,256,256]{2,1,0:T(8,128)(2,1)S(1)} %all-to-all-done, f32[256,8,8]{2,1,0:T(8,128)} %copy.29, f32[256,8,8]{1,2,0:T(8,128)S(1)} %copy.28), kind=kOutput, calls=%fused_computation.27 | convolution fusion | flops 9469952 | bytes 2228224 | tf_op jit(solution)/shard_map/nfh,hne->fne/dot_general | solution.py:35
  42.0 1.2 copy.31
  43.2 5.0 %all-to-all-start.1 = ((bf16[8,256,256]{2,1,0:T(8,128)(2,1)}), bf16[8,256,256]{2,1,0:T(8,128)(2,1)S(1)}, u32[]{:S(2)}, u32[]{:S(2)}) async-start(bf16[8,256,256]{2,1,0:T(8,128)(2,1)} %copy.31), calls=%async_computation.1 | async-start | bytes 2097152 | tf_op jit(solution)/shard_map/all_to_all | solution.py:73
  48.1 9.7 %collective-permute-done = bf16[768,1024]{1,0:T(8,128)(2,1)} collective-permute-done((bf16[768,1024]{1,0:T(8,128)(2,1)}, bf16[768,1024]{1,0:T(8,128)(2,1)}, u32[]{:S(2)}, u32[]{:S(2)}) %collective-permute-start) | collective-permute-done | bytes 1572896 | tf_op jit(solution)/shard_map/ppermute | solution.py:55
  57.8 10.4 %multiply_convert_fusion.1 = (bf16[768,2048]{1,0:T(8,128)(2,1)}, bf16[768,2048]{1,0:T(8,128)(2,1)}) fusion(bf16[768,1024]{1,0:T(8,128)(2,1)} %collective-permute-done, bf16[1,1024,2048]{2,1,0:T(8,128)(2,1)} %param.10), kind=kOutput, calls=%fused_computation.1 | convolution fusion | flops 3236954112 | bytes 12058624 | tf_op jit(solution)/shard_map/dot_general | solution.py:82
  68.2 0.0 all-to-all-done.1
  68.2 0.0 copy-start.3
  68.2 2.0 %fusion.56 = (bf16[768,256]{1,0:T(8,128)(2,1)S(1)}, f32[768,256]{1,0:T(8,128)}) fusion(bf16[2048,256]{1,0:T(8,128)(2,1)S(1)} %bitcast.59, s32[2048]{0:T(1024)S(1)} %bitcast.63), kind=kOutput, calls=%fused_computation.76 | convolution fusion | flops 807075840 | bytes 2236416 | tf_op jit(solution)/shard_map/dot_general | solution.py:76
  70.2 0.0 copy-start.11
  70.2 0.0 copy-start.2
  70.2 0.2 collective-permute-start.1
  70.4 0.0 copy-done.3
  70.4 1.0 multiply_convert_fusion.3
  71.4 0.7 copy-done.11
  72.1 0.4 fusion.25
  72.5 0.0 copy-done.2
  72.5 0.0 copy-start.4
  72.5 1.0 fusion.35
  73.6 6.0 %collective-permute-done.1 = bf16[768,256]{1,0:T(8,128)(2,1)S(1)} collective-permute-done((bf16[768,256]{1,0:T(8,128)(2,1)S(1)}, bf16[768,256]{1,0:T(8,128)(2,1)S(1)}, u32[]{:S(2)}, u32[]{:S(2)}) %collective-permute-start.1) | collective-permute-done | bytes 393248 | tf_op jit(solution)/shard_map/ppermute | solution.py:80
  79.6 0.0 copy-done.4
  79.6 1.0 multiply_convert_fusion
  80.7 0.0 copy-start.5
  80.7 2.2 %fusion.10 = bf16[256,2048]{1,0:T(8,128)(2,1)S(1)} fusion(f32[256,2048]{1,0:T(8,128)S(1)} %fusion.35, bf16[768,2048]{1,0:T(8,128)(2,1)S(1)} %multiply_convert_fusion, bf16[768,1024]{1,0:T(8,128)(2,1)} %collective-permute-done, s32[]{:T(128)S(6)} %select_n.25), kind=kOutput, calls=%fused_computation.23 | convolution fusion | flops 806354944 | bytes 6684676 | tf_op jit(solution)/shard_map/rh,rk->hk/dot_general | solution.py:101
  82.8 0.1 collective-permute-start.2
  82.9 0.0 copy-done.5
  82.9 0.4 fusion.16
  83.4 2.4 %collective-permute-start.3 = (bf16[512,256]{1,0:T(8,128)(2,1)S(1)}, bf16[512,256]{1,0:T(8,128)(2,1)S(1)}, u32[]{:S(2)}, u32[]{:S(2)}) collective-permute-start(bf16[512,256]{1,0:T(8,128)(2,1)S(1)} %fusion.16), channel_id=1, source_target_pairs={{0,2},{1,3},{2,0},{3,1},{4,6},{5,7},{6,4},{7,5},{8,10},{9,11},{10,... | collective-permute-start | bytes 786440 | tf_op jit(solution)/shard_map/ppermute | solution.py:114
  85.8 1.0 fusion.38
  86.8 0.4 fusion.28
  87.2 55.3 %collective-permute-done.3 = bf16[512,256]{1,0:T(8,128)(2,1)S(1)} collective-permute-done((bf16[512,256]{1,0:T(8,128)(2,1)S(1)}, bf16[512,256]{1,0:T(8,128)(2,1)S(1)}, u32[]{:S(2)}, u32[]{:S(2)}) %collective-permute-start.3) | collective-permute-done | bytes 262176 | tf_op jit(solution)/shard_map/ppermute | solution.py:114
  142.5 1.2 fusion.15
  143.7 0.0 collective-permute-done.2
  143.7 3.4 %fusion.9 = f32[1,256,2048]{2,1,0:T(8,128)} fusion(f32[256,2048]{1,0:T(8,128)S(1)} %fusion.38, bf16[768,2048]{1,0:T(8,128)(2,1)S(1)} %multiply_convert_fusion, bf16[256,2048]{1,0:T(8,128)(2,1)S(1)} %collective-permute-done.2, bf16[768,1024]{1,0:T(8,128)(2,1)} %collective-permute-done, s32[]{:T(128)S(6)} %select_n.23), kind=kOutput, calls=%fused_computation.22 | convolution fusion | flops 806879232 | bytes 8781828 | tf_op jit(solution)/shard_map/rh,rk->hk/dot_general | solution.py:101
  (4 shorter events, 0.0 us)
Async XLA Ops:
  0.6 10.3 %copy-start = (bf16[1,2048,256]{2,1,0:T(8,128)(2,1)S(1)}, bf16[1,2048,256]{2,1,0:T(8,128)(2,1)}, u32[]{:S(2)}) copy-start(bf16[1,2048,256]{2,1,0:T(8,128)(2,1)} %param.11) | copy-start | bytes 3145732
  0.6 3.2 %copy-start.9 = (bf16[1,1024,2048]{2,1,0:T(8,128)(2,1)S(1)}, bf16[1,1024,2048]{2,1,0:T(8,128)(2,1)}, u32[]{:S(2)}) copy-start(bf16[1,1024,2048]{2,1,0:T(8,128)(2,1)} %param.10) | copy-start | bytes 12582916
  3.9 7.0 %copy-start.1 = (bf16[768,1024]{1,0:T(8,128)(2,1)}, bf16[768,1024]{1,0:T(8,128)(2,1)S(1)}, u32[]{:S(2)}) copy-start(bf16[768,1024]{1,0:T(8,128)(2,1)S(1)} %fusion.12) | copy-start | bytes 4718596
  3.9 7.0 %copy-start.10 = (s32[1,2048]{1,0:T(1,128)S(1)}, s32[1,2048]{1,0:T(1,128)}, u32[]{:S(2)}) copy-start(s32[1,2048]{1,0:T(1,128)} %param.8) | copy-start | bytes 24580
  10.9 11.1 %copy-start.7 = (bf16[1024]{0:T(1024)(128)(2,1)S(1)}, bf16[1024]{0:T(1024)(128)(2,1)}, u32[]{:S(2)}) copy-start(bf16[1024]{0:T(1024)(128)(2,1)} %param.13) | copy-start | bytes 6148
  10.9 11.2 %copy-start.8 = (s32[256,1]{0,1:T(1,128)S(1)}, s32[256,1]{0,1:T(1,128)}, u32[]{:S(2)}) copy-start(s32[256,1]{0,1:T(1,128)} %param.9) | copy-start | bytes 3076
  17.2 19.7 %copy-start.6 = (bf16[64,1024]{1,0:T(8,128)(2,1)S(1)}, bf16[64,1024]{1,0:T(8,128)(2,1)}, u32[]{:S(2)}) copy-start(bf16[64,1024]{1,0:T(8,128)(2,1)} %param.12) | copy-start | bytes 393220
  17.2 18.6 %all-to-all-start = ((bf16[8,256,256]{2,1,0:T(8,128)(2,1)}), bf16[8,256,256]{2,1,0:T(8,128)(2,1)S(1)}, u32[]{:S(2)}, u32[]{:S(2)}) async-start(bf16[8,256,256]{2,1,0:T(8,128)(2,1)} %bitcast.4), calls=%async_computation | async-start | bytes 2097152 | tf_op jit(solution)/shard_map/all_to_all | solution.py:70
  21.9 35.9 %collective-permute-start = (bf16[768,1024]{1,0:T(8,128)(2,1)}, bf16[768,1024]{1,0:T(8,128)(2,1)}, u32[]{:S(2)}, u32[]{:S(2)}) collective-permute-start(bf16[768,1024]{1,0:T(8,128)(2,1)} %copy-done.1), channel_id=1, source_target_pairs={{0,1},{1,0},{2,3},{3,2},{4,5},{5,4},{6,7},{7,6},{8,9},{9,8},{10,11... | collective-permute-start | bytes 4718600 | tf_op jit(solution)/shard_map/ppermute | solution.py:55
  43.2 25.0 %all-to-all-start.1 = ((bf16[8,256,256]{2,1,0:T(8,128)(2,1)}), bf16[8,256,256]{2,1,0:T(8,128)(2,1)S(1)}, u32[]{:S(2)}, u32[]{:S(2)}) async-start(bf16[8,256,256]{2,1,0:T(8,128)(2,1)} %copy.31), calls=%async_computation.1 | async-start | bytes 2097152 | tf_op jit(solution)/shard_map/all_to_all | solution.py:73
  68.2 2.2 %copy-start.3 = (bf16[768,2048]{1,0:T(8,128)(2,1)S(1)}, bf16[768,2048]{1,0:T(8,128)(2,1)}, u32[]{:S(2)}) copy-start(bf16[768,2048]{1,0:T(8,128)(2,1)} %get-tuple-element.9) | copy-start | bytes 9437188
  70.2 1.9 %copy-start.11 = (bf16[768,2048]{1,0:T(8,128)(2,1)S(1)}, bf16[768,2048]{1,0:T(8,128)(2,1)}, u32[]{:S(2)}) copy-start(bf16[768,2048]{1,0:T(8,128)(2,1)} %get-tuple-element.11) | copy-start | bytes 9437188
  70.2 2.4 %copy-start.2 = (bf16[768,1024]{1,0:T(8,128)(2,1)S(1)}, bf16[768,1024]{1,0:T(8,128)(2,1)}, u32[]{:S(2)}) copy-start(bf16[768,1024]{1,0:T(8,128)(2,1)} %copy-done.1) | copy-start | bytes 4718596
  70.2 9.4 %collective-permute-start.1 = (bf16[768,256]{1,0:T(8,128)(2,1)S(1)}, bf16[768,256]{1,0:T(8,128)(2,1)S(1)}, u32[]{:S(2)}, u32[]{:S(2)}) collective-permute-start(bf16[768,256]{1,0:T(8,128)(2,1)S(1)} %get-tuple-element.17), channel_id=1, source_target_pairs={{0,1},{1,0},{2,3},{3,2},{4,5},{5,4},{6,7},{7,6},{8,9},{9,8},{10,11... | collective-permute-start | bytes 1179656 | tf_op jit(solution)/shard_map/ppermute | solution.py:80
  72.5 7.1 %copy-start.4 = (bf16[768,2048]{1,0:T(8,128)(2,1)S(1)}, bf16[768,2048]{1,0:T(8,128)(2,1)}, u32[]{:S(2)}) copy-start(bf16[768,2048]{1,0:T(8,128)(2,1)} %get-tuple-element.10) | copy-start | bytes 9437188
  80.7 2.3 %copy-start.5 = (bf16[768,2048]{1,0:T(8,128)(2,1)S(1)}, bf16[768,2048]{1,0:T(8,128)(2,1)}, u32[]{:S(2)}) copy-start(bf16[768,2048]{1,0:T(8,128)(2,1)} %get-tuple-element.12) | copy-start | bytes 9437188
  82.8 60.8 %collective-permute-start.2 = (bf16[256,2048]{1,0:T(8,128)(2,1)S(1)}, bf16[256,2048]{1,0:T(8,128)(2,1)S(1)}, u32[]{:S(2)}, u32[]{:S(2)}) collective-permute-start(bf16[256,2048]{1,0:T(8,128)(2,1)S(1)} %fusion.10), channel_id=1, source_target_pairs={{0,2},{1,3},{2,0},{3,1},{4,6},{5,7},{6,4},{7,5},{8,10},{9,11},{10,... | collective-permute-start | bytes 3145736 | tf_op jit(solution)/shard_map/ppermute | solution.py:112
  83.4 59.1 %collective-permute-start.3 = (bf16[512,256]{1,0:T(8,128)(2,1)S(1)}, bf16[512,256]{1,0:T(8,128)(2,1)S(1)}, u32[]{:S(2)}, u32[]{:S(2)}) collective-permute-start(bf16[512,256]{1,0:T(8,128)(2,1)S(1)} %fusion.16), channel_id=1, source_target_pairs={{0,2},{1,3},{2,0},{3,1},{4,6},{5,7},{6,4},{7,5},{8,10},{9,11},{10,... | collective-permute-start | bytes 786440 | tf_op jit(solution)/shard_map/ppermute | solution.py:114

commit v3 on v2

--- a/solution.py
+++ b/solution.py
@@ -53,11 +53,15 @@
     slot_count = encoded.shape[0]
     encoded = lax.optimization_barrier(encoded)
     encoded_far = lax.ppermute(encoded, "samp", across)
-    first_pre = jnp.dot(encoded, weight_first, preferred_element_type=jnp.float32)
-    first_hidden = jax.nn.silu(first_pre).astype(jnp.bfloat16)
-    slope = silu_slope(first_pre).astype(jnp.bfloat16)
-    row_table = jnp.dot(first_hidden, weight_second, preferred_element_type=jnp.float32).astype(
-        jnp.bfloat16
+
+    def hidden_of(codes):
+        first_pre = jnp.dot(codes, weight_first, preferred_element_type=jnp.float32)
+        return jax.nn.silu(first_pre).astype(jnp.bfloat16), silu_slope(first_pre).astype(jnp.bfloat16)
+
+    row_table = lax.optimization_barrier(
+        jnp.dot(
+            hidden_of(encoded)[0], weight_second, preferred_element_type=jnp.float32
+        ).astype(jnp.bfloat16)
     )
     positions = sample_index[0]
     slots = lax.broadcasted_iota(jnp.int32, (positions.shape[0], slot_count), 1)
@@ -67,9 +71,13 @@
         .astype(jnp.bfloat16)
         .reshape(feat_count, -1, emb_width)
     )
+    chosen_rows, encoded = lax.optimization_barrier((chosen_rows, encoded))
+    first_hidden, slope = hidden_of(encoded)
     picked = lax.all_to_all(chosen_rows, "feat", split_axis=0, concat_axis=0, tiled=True)
+    picked, encoded_far, slope, first_hidden = lax.optimization_barrier(
+        (picked, encoded_far, slope, first_hidden)
+    )
     emb_delta = top_tower(picked, labels[:, 0], top_weight, score_vector)
-    emb_delta, slope, first_hidden = lax.optimization_barrier((emb_delta, slope, first_hidden))
     returned = lax.all_to_all(emb_delta, "feat", split_axis=0, concat_axis=0, tiled=True)
     slots_back = lax.broadcasted_iota(jnp.int32, (slot_count, positions.shape[0]), 0)
     placer = (positions[None, :] == slots_back).astype(jnp.bfloat16)

time: 149 us -> 149 us (level)
  matrix products: 41.8 us -> 50.3 us
  waiting for transfers between devices: 84.7 us -> 77.1 us
    dot_general x1 -> x2, matrix products: 7.02 us -> 17.4 us  [the longest x1 10.4 us: hidden_of(): first_pre = jnp.dot(codes, weight_first, preferred_element_type=jnp.float32)]
    all_to_all x1, waiting for transfers between devices: 13.7 us -> 3.44 us  [local(): lax.all_to_all(chosen_rows, 'feat', split_axis=0, concat_axis=0, tiled=True)]
    dot_general x1, matrix products: 6.24 us -> 2.26 us  [local(): jnp.dot(chooser, row_table, preferred_element_type=jnp.float32)]
    all_to_all x1, waiting for transfers between devices: 0.01 us -> 3.47 us  [local(): lax.all_to_all(emb_delta, 'feat', split_axis=0, concat_axis=0, tiled=True)]
    ppermute x1, waiting for transfers between devices: 6.05 us -> 9.06 us  [local(): row_delta_far = lax.ppermute(row_delta, 'samp', across)]
    ppermute x1, waiting for transfers between devices: 9.68 us -> 7.29 us  [local(): encoded_far = lax.ppermute(encoded, 'samp', across)]
    dot_general x4, matrix products: 7.56 us -> 9.71 us  [first_part(): jnp.einsum('rh,rk->hk', columns, group[3], preferred_element_type=jnp.flo...]
  transfers between devices with their start and end apart: 6 -> 6, of which waited for: 4 -> 5; matrix products, arithmetic and copies ran while one was open for 16% -> 24% of each run, Pallas kernels for 0% -> 0%
where the time goes in v3:
time: 149 us; the launch traced here: 148 us
  waiting for transfers between devices  77.1 us (52%)
  matrix products  50.3 us (34%)
  starting transfers between devices  12.9 us (9%)
  other arithmetic  3.66 us (2%)
  local copies, waits for them, and re-layouts  3.55 us (2%)
    ppermute x1, waiting for transfers between devices, local(): seconds.append(lax.ppermute(second_out, 'samp', pairs))  53.8 us
    dot_general x1, matrix products, hidden_of(): first_pre = jnp.dot(codes, weight_first, preferred_element_type=jnp.float32)  10.4 us
    dot_general x1, matrix products, local(): jnp.dot(encoded_far, weight_first, preferred_element_type=jnp.float32)  10.4 us
    dot_general x4, matrix products, first_part(): jnp.einsum('rh,rk->hk', columns, group[3], preferred_element_type=jnp.flo...  9.71 us
    ppermute x1, waiting for transfers between devices, local(): row_delta_far = lax.ppermute(row_delta, 'samp', across)  9.06 us
    ppermute x1, waiting for transfers between devices, local(): encoded_far = lax.ppermute(encoded, 'samp', across)  7.29 us
    dot_general x1, matrix products, local(): jnp.dot(hidden_of(encoded)[0], weight_second, preferred_element_type=jnp....  7.03 us
    all_to_all x1, starting transfers between devices, local(): lax.all_to_all(emb_delta, 'feat', split_axis=0, concat_axis=0, tiled=True)  5.44 us
  transfers between devices with their start and end apart: 6, of which 5 were waited for; matrix products, arithmetic and copies ran while one was open for 24% of the time, Pallas kernels for 0%

profile of v3, /device:TPU:27, one launch (start us, length us, event | category | flops | bytes accessed | tf_op | source)
XLA Modules:
  0.0 148.3 jit_solution(2175009790751645339)
XLA Ops:
  0.6 0.0 copy-start
  0.6 3.6 %fusion.16 = bf16[768,1024]{1,0:T(8,128)(2,1)} fusion(s32[1,768,1024]{2,1,0:T(8,128)} %param.7), kind=kLoop, calls=%fused_computation.27 | loop fusion | flops 3145728 | bytes 4718592 | tf_op jit(solution)/shard_map/convert_element_type | solution.py:52
  4.3 0.0 copy-start.7
  4.3 0.2 collective-permute-start
  4.5 0.0 copy-done
  4.5 7.0 %fusion.18 = bf16[768,256]{1,0:T(8,128)(2,1)S(1)} fusion(bf16[768,1024]{1,0:T(8,128)(2,1)} %fusion.16, bf16[1,1024,2048]{2,1,0:T(8,128)(2,1)} %param.10, bf16[1,2048,256]{2,1,0:T(8,128)(2,1)S(1)} %copy-done), kind=kOutput, calls=%fused_computation.29 | convolution fusion | flops 4034592768 | bytes 7208960 | tf_op jit(solution)/shard_map/dot_general | solution.py:62
  11.5 0.0 copy-done.7
  11.5 0.0 copy-start.5
  11.5 0.0 copy-start.6
  11.5 2.3 %fusion.11 = bf16[2048,256]{1,0:T(8,128)(2,1)} fusion(bf16[768,256]{1,0:T(8,128)(2,1)S(1)} %fusion.18, s32[2048]{0:T(1024)S(1)} %bitcast.67), kind=kOutput, calls=%fused_computation.23 | convolution fusion | flops 807403520 | bytes 1449984 | tf_op jit(solution)/shard_map/dot_general | solution.py:70
  13.8 4.8 %all-to-all-start = ((bf16[8,256,256]{2,1,0:T(8,128)(2,1)}), bf16[8,256,256]{2,1,0:T(8,128)(2,1)S(1)}, u32[]{:S(2)}, u32[]{:S(2)}) async-start(bf16[8,256,256]{2,1,0:T(8,128)(2,1)} %bitcast.4), calls=%async_computation | async-start | bytes 2097152 | tf_op jit(solution)/shard_map/all_to_all | solution.py:76
  18.6 0.0 copy-done.5
  18.7 0.0 copy-done.6
  18.7 10.4 %multiply_convert_fusion.4 = (bf16[768,2048]{1,0:T(8,128)(2,1)}, bf16[768,2048]{1,0:T(8,128)(2,1)}) fusion(bf16[768,1024]{1,0:T(8,128)(2,1)} %fusion.16, bf16[1,1024,2048]{2,1,0:T(8,128)(2,1)} %param.10), kind=kOutput, calls=%fused_computation.5 | convolution fusion | flops 3236954112 | bytes 12058624 | tf_op jit(solution)/shard_map/dot_general | solution.py:58
  29.1 0.0 copy-start.4
  29.1 3.4 %all-to-all-done = bf16[8,256,256]{2,1,0:T(8,128)(2,1)S(1)} async-done(((bf16[8,256,256]{2,1,0:T(8,128)(2,1)}), bf16[8,256,256]{2,1,0:T(8,128)(2,1)S(1)}, u32[]{:S(2)}, u32[]{:S(2)}) %all-to-all-start) | async-done | bytes 1048608 | tf_op jit(solution)/shard_map/all_to_all | solution.py:76
  32.6 7.3 %collective-permute-done = bf16[768,1024]{1,0:T(8,128)(2,1)} collective-permute-done((bf16[768,1024]{1,0:T(8,128)(2,1)}, bf16[768,1024]{1,0:T(8,128)(2,1)}, u32[]{:S(2)}, u32[]{:S(2)}) %collective-permute-start) | collective-permute-done | bytes 1572896 | tf_op jit(solution)/shard_map/ppermute | solution.py:55
  39.9 0.7 fusion.29
  40.6 0.4 copy.27
  40.9 0.0 copy-done.4
  40.9 0.3 fusion.53
  41.3 0.4 fusion.39
  41.7 0.6 convolution_bitcast_fusion
  42.2 0.4 copy.28
  42.7 1.3 copy.29
  44.0 2.0 %fusion.17 = bf16[8,256,256]{2,0,1:T(8,128)(2,1)S(1)} fusion(bf16[8,256,256]{2,1,0:T(8,128)(2,1)S(1)} %all-to-all-done, f32[256,8,8]{2,1,0:T(8,128)} %copy.29, f32[256,8,8]{1,2,0:T(8,128)S(1)} %copy.28), kind=kOutput, calls=%fused_computation.28 | convolution fusion | flops 9469952 | bytes 2228224 | tf_op jit(solution)/shard_map/nfh,hne->fne/dot_general | solution.py:35
  46.0 1.2 copy.31
  47.2 5.4 %all-to-all-start.1 = ((bf16[8,256,256]{2,1,0:T(8,128)(2,1)}), bf16[8,256,256]{2,1,0:T(8,128)(2,1)S(1)}, u32[]{:S(2)}, u32[]{:S(2)}) async-start(bf16[8,256,256]{2,1,0:T(8,128)(2,1)} %copy.31), calls=%async_computation.1 | async-start | bytes 2097152 | tf_op jit(solution)/shard_map/all_to_all | solution.py:81
  52.6 10.4 %multiply_convert_fusion.1 = (bf16[768,2048]{1,0:T(8,128)(2,1)}, bf16[768,2048]{1,0:T(8,128)(2,1)}) fusion(bf16[768,1024]{1,0:T(8,128)(2,1)} %collective-permute-done, bf16[1,1024,2048]{2,1,0:T(8,128)(2,1)} %param.10), kind=kOutput, calls=%fused_computation.1 | convolution fusion | flops 3236954112 | bytes 12058624 | tf_op jit(solution)/shard_map/dot_general | solution.py:90
  63.0 3.5 %all-to-all-done.1 = bf16[8,256,256]{2,1,0:T(8,128)(2,1)S(1)} async-done(((bf16[8,256,256]{2,1,0:T(8,128)(2,1)}), bf16[8,256,256]{2,1,0:T(8,128)(2,1)S(1)}, u32[]{:S(2)}, u32[]{:S(2)}) %all-to-all-start.1) | async-done | bytes 1048608 | tf_op jit(solution)/shard_map/all_to_all | solution.py:81
  66.4 2.0 %fusion.69 = (bf16[768,256]{1,0:T(8,128)(2,1)S(1)}, f32[768,256]{1,0:T(8,128)}) fusion(bf16[2048,256]{1,0:T(8,128)(2,1)S(1)} %bitcast.64, s32[2048]{0:T(1024)S(1)} %bitcast.68), kind=kOutput, calls=%fused_computation.81 | convolution fusion | flops 807075840 | bytes 2236416 | tf_op jit(solution)/shard_map/dot_general | solution.py:84
  68.4 0.0 copy-start.2
  68.4 0.2 collective-permute-start.1
  68.6 1.0 fusion.26
  69.6 9.1 %collective-permute-done.1 = bf16[768,256]{1,0:T(8,128)(2,1)S(1)} collective-permute-done((bf16[768,256]{1,0:T(8,128)(2,1)S(1)}, bf16[768,256]{1,0:T(8,128)(2,1)S(1)}, u32[]{:S(2)}, u32[]{:S(2)}) %collective-permute-start.1) | collective-permute-done | bytes 393248 | tf_op jit(solution)/shard_map/ppermute | solution.py:88
  78.7 0.0 copy-done.2
  78.7 1.0 multiply_convert_fusion
  79.7 0.0 copy-start.1
  79.7 2.1 %fusion.40 = f32[256,2048]{1,0:T(8,128)S(1)} fusion(bf16[768,2048]{1,0:T(8,128)(2,1)S(1)} %multiply_convert_fusion, bf16[768,1024]{1,0:T(8,128)(2,1)} %collective-permute-done, s32[]{:T(128)S(6)} %select_n.25), kind=kOutput, calls=%fused_computation.55 | convolution fusion | flops 805306368 | bytes 5636100 | tf_op jit(solution)/shard_map/rh,rk->hk/dot_general | solution.py:109
  81.9 0.0 copy-done.1
  81.9 0.0 copy-start.8
  81.9 0.0 copy-start.3
  81.9 2.2 %add_convert_fusion.1 = bf16[256,2048]{1,0:T(8,128)(2,1)S(1)} fusion(f32[256,2048]{1,0:T(8,128)S(1)} %fusion.40, bf16[768,1024]{1,0:T(8,128)(2,1)} %fusion.16, s32[]{:T(128)S(6)} %select_n.25, f32[768,2048]{1,0:T(8,128)S(1)} %fusion.26, bf16[768,2048]{1,0:T(8,128)(2,1)S(1)} %copy-done.1), kind=kOutput, calls=%fused_computation.25 | convolution fusion | flops 811073536 | bytes 12976132 | tf_op jit(solution)/shard_map/rh,rk->hk/dot_general | solution.py:109
  84.1 0.1 collective-permute-start.2
  84.2 0.0 copy-done.8
  84.2 0.4 fusion.32
  84.6 0.2 copy-done.3
  84.9 0.4 fusion.23
  85.3 2.2 %collective-permute-start.3 = (bf16[512,256]{1,0:T(8,128)(2,1)S(1)}, bf16[512,256]{1,0:T(8,128)(2,1)S(1)}, u32[]{:S(2)}, u32[]{:S(2)}) collective-permute-start(bf16[512,256]{1,0:T(8,128)(2,1)S(1)} %fusion.23), channel_id=1, source_target_pairs={{0,2},{1,3},{2,0},{3,1},{4,6},{5,7},{6,4},{7,5},{8,10},{9,11},{10,... | collective-permute-start | bytes 786440 | tf_op jit(solution)/shard_map/ppermute | solution.py:122
  87.5 2.0 %fusion.46 = f32[256,2048]{1,0:T(8,128)S(1)} fusion(bf16[768,2048]{1,0:T(8,128)(2,1)S(1)} %multiply_convert_fusion, bf16[768,1024]{1,0:T(8,128)(2,1)} %collective-permute-done, s32[]{:T(128)S(6)} %select_n.23), kind=kOutput, calls=%fused_computation.59 | convolution fusion | flops 805306368 | bytes 5636100 | tf_op jit(solution)/shard_map/rh,rk->hk/dot_general | solution.py:109
  89.5 0.4 fusion.35
  89.9 53.8 %collective-permute-done.3 = bf16[512,256]{1,0:T(8,128)(2,1)S(1)} collective-permute-done((bf16[512,256]{1,0:T(8,128)(2,1)S(1)}, bf16[512,256]{1,0:T(8,128)(2,1)S(1)}, u32[]{:S(2)}, u32[]{:S(2)}) %collective-permute-start.3) | collective-permute-done | bytes 262176 | tf_op jit(solution)/shard_map/ppermute | solution.py:122
  143.7 1.2 fusion.22
  144.9 0.0 collective-permute-done.2
  144.9 3.4 %add_bitcast_fusion = f32[1,256,2048]{2,1,0:T(8,128)} fusion(bf16[256,2048]{1,0:T(8,128)(2,1)S(1)} %collective-permute-done.2, f32[256,2048]{1,0:T(8,128)S(1)} %fusion.46, bf16[768,1024]{1,0:T(8,128)(2,1)} %fusion.16, s32[]{:T(128)S(6)} %select_n.23, f32[768,2048]{1,0:T(8,128)S(1)} %fusion.26, bf16[768,2048]{1,0:T(8,128)(2,1)S(1)} %copy-done.1), kind=kOutput, calls=%fused_computation.24 | convolution fusion | flops 811597824 | bytes 15073284 | tf_op jit(solution)/shard_map/rh,rk->hk/dot_general | solution.py:109
  (4 shorter events, 0.0 us)
Async XLA Ops:
  0.6 3.8 %copy-start = (bf16[1,2048,256]{2,1,0:T(8,128)(2,1)S(1)}, bf16[1,2048,256]{2,1,0:T(8,128)(2,1)}, u32[]{:S(2)}) copy-start(bf16[1,2048,256]{2,1,0:T(8,128)(2,1)} %param.11) | copy-start | bytes 3145732
  4.3 7.2 %copy-start.7 = (s32[1,2048]{1,0:T(1,128)S(1)}, s32[1,2048]{1,0:T(1,128)}, u32[]{:S(2)}) copy-start(s32[1,2048]{1,0:T(1,128)} %param.8) | copy-start | bytes 24580
  4.3 35.6 %collective-permute-start = (bf16[768,1024]{1,0:T(8,128)(2,1)}, bf16[768,1024]{1,0:T(8,128)(2,1)}, u32[]{:S(2)}, u32[]{:S(2)}) collective-permute-start(bf16[768,1024]{1,0:T(8,128)(2,1)} %fusion.16), channel_id=1, source_target_pairs={{0,1},{1,0},{2,3},{3,2},{4,5},{5,4},{6,7},{7,6},{8,9},{9,8},{10,11... | collective-permute-start | bytes 4718600 | tf_op jit(solution)/shard_map/ppermute | solution.py:55
  11.5 7.1 %copy-start.5 = (bf16[1024]{0:T(1024)(128)(2,1)S(1)}, bf16[1024]{0:T(1024)(128)(2,1)}, u32[]{:S(2)}) copy-start(bf16[1024]{0:T(1024)(128)(2,1)} %param.13) | copy-start | bytes 6148
  11.5 7.2 %copy-start.6 = (s32[256,1]{0,1:T(1,128)S(1)}, s32[256,1]{0,1:T(1,128)}, u32[]{:S(2)}) copy-start(s32[256,1]{0,1:T(1,128)} %param.9) | copy-start | bytes 3076
  13.8 18.8 %all-to-all-start = ((bf16[8,256,256]{2,1,0:T(8,128)(2,1)}), bf16[8,256,256]{2,1,0:T(8,128)(2,1)S(1)}, u32[]{:S(2)}, u32[]{:S(2)}) async-start(bf16[8,256,256]{2,1,0:T(8,128)(2,1)} %bitcast.4), calls=%async_computation | async-start | bytes 2097152 | tf_op jit(solution)/shard_map/all_to_all | solution.py:76
  29.1 11.8 %copy-start.4 = (bf16[64,1024]{1,0:T(8,128)(2,1)S(1)}, bf16[64,1024]{1,0:T(8,128)(2,1)}, u32[]{:S(2)}) copy-start(bf16[64,1024]{1,0:T(8,128)(2,1)} %param.12) | copy-start | bytes 393220
  47.2 19.3 %all-to-all-start.1 = ((bf16[8,256,256]{2,1,0:T(8,128)(2,1)}), bf16[8,256,256]{2,1,0:T(8,128)(2,1)S(1)}, u32[]{:S(2)}, u32[]{:S(2)}) async-start(bf16[8,256,256]{2,1,0:T(8,128)(2,1)} %copy.31), calls=%async_computation.1 | async-start | bytes 2097152 | tf_op jit(solution)/shard_map/all_to_all | solution.py:81
  68.4 10.3 %copy-start.2 = (bf16[768,2048]{1,0:T(8,128)(2,1)S(1)}, bf16[768,2048]{1,0:T(8,128)(2,1)}, u32[]{:S(2)}) copy-start(bf16[768,2048]{1,0:T(8,128)(2,1)} %get-tuple-element.16) | copy-start | bytes 9437188
  68.4 10.2 %collective-permute-start.1 = (bf16[768,256]{1,0:T(8,128)(2,1)S(1)}, bf16[768,256]{1,0:T(8,128)(2,1)S(1)}, u32[]{:S(2)}, u32[]{:S(2)}) collective-permute-start(bf16[768,256]{1,0:T(8,128)(2,1)S(1)} %get-tuple-element.23), channel_id=1, source_target_pairs={{0,1},{1,0},{2,3},{3,2},{4,5},{5,4},{6,7},{7,6},{8,9},{9,8},{10,11... | collective-permute-start | bytes 1179656 | tf_op jit(solution)/shard_map/ppermute | solution.py:88
  79.7 2.2 %copy-start.1 = (bf16[768,2048]{1,0:T(8,128)(2,1)S(1)}, bf16[768,2048]{1,0:T(8,128)(2,1)}, u32[]{:S(2)}) copy-start(bf16[768,2048]{1,0:T(8,128)(2,1)} %get-tuple-element.14) | copy-start | bytes 9437188
  81.9 2.3 %copy-start.8 = (bf16[768,2048]{1,0:T(8,128)(2,1)S(1)}, bf16[768,2048]{1,0:T(8,128)(2,1)}, u32[]{:S(2)}) copy-start(bf16[768,2048]{1,0:T(8,128)(2,1)} %get-tuple-element.18) | copy-start | bytes 9437188
  81.9 3.0 %copy-start.3 = (bf16[768,2048]{1,0:T(8,128)(2,1)S(1)}, bf16[768,2048]{1,0:T(8,128)(2,1)}, u32[]{:S(2)}) copy-start(bf16[768,2048]{1,0:T(8,128)(2,1)} %get-tuple-element.17) | copy-start | bytes 9437188
  84.1 60.9 %collective-permute-start.2 = (bf16[256,2048]{1,0:T(8,128)(2,1)S(1)}, bf16[256,2048]{1,0:T(8,128)(2,1)S(1)}, u32[]{:S(2)}, u32[]{:S(2)}) collective-permute-start(bf16[256,2048]{1,0:T(8,128)(2,1)S(1)} %add_convert_fusion.1), channel_id=1, source_target_pairs={{0,2},{1,3},{2,0},{3,1},{4,6},{5,7},{6,4},{7,5},{8,10},{9,11},{10,... | collective-permute-start | bytes 3145736 | tf_op jit(solution)/shard_map/ppermute | solution.py:120
  85.3 58.4 %collective-permute-start.3 = (bf16[512,256]{1,0:T(8,128)(2,1)S(1)}, bf16[512,256]{1,0:T(8,128)(2,1)S(1)}, u32[]{:S(2)}, u32[]{:S(2)}) collective-permute-start(bf16[512,256]{1,0:T(8,128)(2,1)S(1)} %fusion.23), channel_id=1, source_target_pairs={{0,2},{1,3},{2,0},{3,1},{4,6},{5,7},{6,4},{7,5},{8,10},{9,11},{10,... | collective-permute-start | bytes 786440 | tf_op jit(solution)/shard_map/ppermute | solution.py:122

commit v4 on v3

--- a/solution.py
+++ b/solution.py
@@ -74,10 +74,9 @@
     chosen_rows, encoded = lax.optimization_barrier((chosen_rows, encoded))
     first_hidden, slope = hidden_of(encoded)
     picked = lax.all_to_all(chosen_rows, "feat", split_axis=0, concat_axis=0, tiled=True)
-    picked, encoded_far, slope, first_hidden = lax.optimization_barrier(
-        (picked, encoded_far, slope, first_hidden)
-    )
+    picked, slope, first_hidden = lax.optimization_barrier((picked, slope, first_hidden))
     emb_delta = top_tower(picked, labels[:, 0], top_weight, score_vector)
+    emb_delta, encoded_far = lax.optimization_barrier((emb_delta, encoded_far))
     returned = lax.all_to_all(emb_delta, "feat", split_axis=0, concat_axis=0, tiled=True)
     slots_back = lax.broadcasted_iota(jnp.int32, (slot_count, positions.shape[0]), 0)
     placer = (positions[None, :] == slots_back).astype(jnp.bfloat16)

time: 149 us -> 140 us (0.940)
  waiting for transfers between devices: 77.1 us -> 68.1 us
    ppermute x1, waiting for transfers between devices: 7.29 us -> 1.14 us  [local(): encoded_far = lax.ppermute(encoded, 'samp', across)]
    ppermute x1, waiting for transfers between devices: 9.06 us -> 5.79 us  [local(): row_delta_far = lax.ppermute(row_delta, 'samp', across)]
  transfers between devices with their start and end apart: 6 -> 6, of which waited for: 5 -> 5; matrix products, arithmetic and copies ran while one was open for 24% -> 31% of each run, Pallas kernels for 0% -> 0%
where the time goes in v4:
time: 140 us
  waiting for transfers between devices  68.1 us (49%)
  matrix products  50.2 us (36%)
  starting transfers between devices  13.1 us (9%)
  local copies, waits for them, and re-layouts  4.02 us (3%)
  other arithmetic  3.61 us (3%)
    ppermute x1, waiting for transfers between devices, local(): seconds.append(lax.ppermute(second_out, 'samp', pairs))  54.3 us
    dot_general x1, matrix products, hidden_of(): first_pre = jnp.dot(codes, weight_first, preferred_element_type=jnp.float32)  10.4 us
    dot_general x1, matrix products, local(): jnp.dot(encoded_far, weight_first, preferred_element_type=jnp.float32)  10.4 us
    dot_general x4, matrix products, first_part(): jnp.einsum('rh,rk->hk', columns, group[3], preferred_element_type=jnp.flo...  9.65 us
    dot_general x1, matrix products, local(): jnp.dot(hidden_of(encoded)[0], weight_second, preferred_element_type=jnp....  7.03 us
    ppermute x1, waiting for transfers between devices, local(): row_delta_far = lax.ppermute(row_delta, 'samp', across)  5.79 us
    all_to_all x1, starting transfers between devices, local(): lax.all_to_all(emb_delta, 'feat', split_axis=0, concat_axis=0, tiled=True)  5.44 us
    all_to_all x1, starting transfers between devices, local(): lax.all_to_all(chosen_rows, 'feat', split_axis=0, concat_axis=0, tiled=True)  4.85 us
  transfers between devices with their start and end apart: 6, of which 5 were waited for; matrix products, arithmetic and copies ran while one was open for 31% of the time, Pallas kernels for 0%

profile of v4, /device:TPU:27, one launch (start us, length us, event | category | flops | bytes accessed | tf_op | source)
XLA Modules:
  0.0 139.9 jit_solution(6380959585036536897)
XLA Ops:
  0.6 0.0 copy-start
  0.6 3.6 %fusion.19 = bf16[768,1024]{1,0:T(8,128)(2,1)} fusion(s32[1,768,1024]{2,1,0:T(8,128)} %param.7), kind=kLoop, calls=%fused_computation.30 | loop fusion | flops 3145728 | bytes 4718592 | tf_op jit(solution)/shard_map/convert_element_type | solution.py:52
  4.2 0.0 copy-start.7
  4.2 0.2 collective-permute-start
  4.4 0.0 copy-done
  4.4 7.0 %fusion.21 = bf16[768,256]{1,0:T(8,128)(2,1)S(1)} fusion(bf16[768,1024]{1,0:T(8,128)(2,1)} %fusion.19, bf16[1,1024,2048]{2,1,0:T(8,128)(2,1)} %param.10, bf16[1,2048,256]{2,1,0:T(8,128)(2,1)S(1)} %copy-done), kind=kOutput, calls=%fused_computation.32 | convolution fusion | flops 4034592768 | bytes 7208960 | tf_op jit(solution)/shard_map/dot_general | solution.py:62
  11.5 0.0 copy-done.7
  11.5 0.0 copy-start.5
  11.5 0.0 copy-start.6
  11.5 2.3 %fusion.14 = bf16[2048,256]{1,0:T(8,128)(2,1)} fusion(bf16[768,256]{1,0:T(8,128)(2,1)S(1)} %fusion.21, s32[2048]{0:T(1024)S(1)} %bitcast.69), kind=kOutput, calls=%fused_computation.28 | convolution fusion | flops 807403520 | bytes 1449984 | tf_op jit(solution)/shard_map/dot_general | solution.py:70
  13.7 4.9 %all-to-all-start = ((bf16[8,256,256]{2,1,0:T(8,128)(2,1)}), bf16[8,256,256]{2,1,0:T(8,128)(2,1)S(1)}, u32[]{:S(2)}, u32[]{:S(2)}) async-start(bf16[8,256,256]{2,1,0:T(8,128)(2,1)} %bitcast.4), calls=%async_computation | async-start | bytes 2097152 | tf_op jit(solution)/shard_map/all_to_all | solution.py:76
  18.6 0.0 copy-done.5
  18.6 0.0 copy-done.6
  18.7 10.4 %multiply_convert_fusion.4 = (bf16[768,2048]{1,0:T(8,128)(2,1)}, bf16[768,2048]{1,0:T(8,128)(2,1)}) fusion(bf16[768,1024]{1,0:T(8,128)(2,1)} %fusion.19, bf16[1,1024,2048]{2,1,0:T(8,128)(2,1)} %param.10), kind=kOutput, calls=%fused_computation.5 | convolution fusion | flops 3236954112 | bytes 12058624 | tf_op jit(solution)/shard_map/dot_general | solution.py:58
  29.1 0.0 copy-start.4
  29.1 3.5 %all-to-all-done = bf16[8,256,256]{2,1,0:T(8,128)(2,1)S(1)} async-done(((bf16[8,256,256]{2,1,0:T(8,128)(2,1)}), bf16[8,256,256]{2,1,0:T(8,128)(2,1)S(1)}, u32[]{:S(2)}, u32[]{:S(2)}) %all-to-all-start) | async-done | bytes 1048608 | tf_op jit(solution)/shard_map/all_to_all | solution.py:76
  32.5 0.7 fusion.31
  33.2 0.4 copy.27
  33.6 0.0 copy-done.4
  33.6 0.3 fusion.49
  33.9 0.4 fusion.41
  34.3 0.6 convolution_bitcast_fusion
  34.9 0.4 copy.29
  35.3 1.3 copy.28
  36.7 2.0 %fusion.20 = bf16[8,256,256]{2,0,1:T(8,128)(2,1)S(1)} fusion(bf16[8,256,256]{2,1,0:T(8,128)(2,1)S(1)} %all-to-all-done, f32[256,8,8]{2,1,0:T(8,128)S(1)} %copy.29, f32[256,8,8]{1,2,0:T(8,128)} %copy.28), kind=kOutput, calls=%fused_computation.31 | convolution fusion | flops 9469952 | bytes 2228224 | tf_op jit(solution)/shard_map/nfh,hne->fne/dot_general | solution.py:35
  38.7 1.1 collective-permute-done
  39.8 1.2 copy.31
  41.0 5.4 %all-to-all-start.1 = ((bf16[8,256,256]{2,1,0:T(8,128)(2,1)}), bf16[8,256,256]{2,1,0:T(8,128)(2,1)S(1)}, u32[]{:S(2)}, u32[]{:S(2)}) async-start(bf16[8,256,256]{2,1,0:T(8,128)(2,1)} %copy.31), calls=%async_computation.1 | async-start | bytes 2097152 | tf_op jit(solution)/shard_map/all_to_all | solution.py:80
  46.4 10.4 %multiply_convert_fusion.1 = (bf16[768,2048]{1,0:T(8,128)(2,1)}, bf16[768,2048]{1,0:T(8,128)(2,1)}) fusion(bf16[768,1024]{1,0:T(8,128)(2,1)} %collective-permute-done, bf16[1,1024,2048]{2,1,0:T(8,128)(2,1)} %param.10), kind=kOutput, calls=%fused_computation.1 | convolution fusion | flops 3236954112 | bytes 12058624 | tf_op jit(solution)/shard_map/dot_general | solution.py:89
  56.8 3.4 %all-to-all-done.1 = bf16[8,256,256]{2,1,0:T(8,128)(2,1)S(1)} async-done(((bf16[8,256,256]{2,1,0:T(8,128)(2,1)}), bf16[8,256,256]{2,1,0:T(8,128)(2,1)S(1)}, u32[]{:S(2)}, u32[]{:S(2)}) %all-to-all-start.1) | async-done | bytes 1048608 | tf_op jit(solution)/shard_map/all_to_all | solution.py:80
  60.2 0.0 copy-start.1
  60.3 2.0 %fusion.65 = (bf16[768,256]{1,0:T(8,128)(2,1)S(1)}, f32[768,256]{1,0:T(8,128)}) fusion(bf16[2048,256]{1,0:T(8,128)(2,1)S(1)} %bitcast.66, s32[2048]{0:T(1024)S(1)} %bitcast.70), kind=kOutput, calls=%fused_computation.81 | convolution fusion | flops 807075840 | bytes 2236416 | tf_op jit(solution)/shard_map/dot_general | solution.py:83
  62.2 0.0 copy-start.8
  62.2 0.2 collective-permute-start.1
  62.4 0.0 copy-done.1
  62.4 1.0 multiply_convert_fusion.3
  63.4 0.7 copy-done.8
  64.1 0.4 fusion.35
  64.5 0.0 copy-start.2
  64.6 2.1 %fusion.43 = f32[256,2048]{1,0:T(8,128)S(1)} fusion(bf16[768,2048]{1,0:T(8,128)(2,1)S(1)} %multiply_convert_fusion.3, bf16[768,1024]{1,0:T(8,128)(2,1)} %fusion.19, s32[]{:T(128)S(6)} %select_n.25), kind=kOutput, calls=%fused_computation.58 | convolution fusion | flops 805306368 | bytes 5636100 | tf_op jit(solution)/shard_map/rh,rk->hk/dot_general | solution.py:108
  66.7 5.8 %collective-permute-done.1 = bf16[768,256]{1,0:T(8,128)(2,1)S(1)} collective-permute-done((bf16[768,256]{1,0:T(8,128)(2,1)S(1)}, bf16[768,256]{1,0:T(8,128)(2,1)S(1)}, u32[]{:S(2)}, u32[]{:S(2)}) %collective-permute-start.1) | collective-permute-done | bytes 393248 | tf_op jit(solution)/shard_map/ppermute | solution.py:87
  72.5 0.0 copy-done.2
  72.5 1.0 multiply_convert_fusion
  73.5 0.0 copy-start.3
  73.5 2.2 %fusion.13 = bf16[256,2048]{1,0:T(8,128)(2,1)S(1)} fusion(f32[256,2048]{1,0:T(8,128)S(1)} %fusion.43, bf16[768,2048]{1,0:T(8,128)(2,1)S(1)} %multiply_convert_fusion, bf16[768,1024]{1,0:T(8,128)(2,1)} %collective-permute-done, s32[]{:T(128)S(6)} %select_n.25), kind=kOutput, calls=%fused_computation.27 | convolution fusion | flops 806354944 | bytes 6684676 | tf_op jit(solution)/shard_map/rh,rk->hk/dot_general | solution.py:108
  75.7 0.1 collective-permute-start.2
  75.8 0.0 copy-done.3
  75.8 0.4 fusion.26
  76.2 2.4 %collective-permute-start.3 = (bf16[512,256]{1,0:T(8,128)(2,1)S(1)}, bf16[512,256]{1,0:T(8,128)(2,1)S(1)}, u32[]{:S(2)}, u32[]{:S(2)}) collective-permute-start(bf16[512,256]{1,0:T(8,128)(2,1)S(1)} %fusion.26), channel_id=1, source_target_pairs={{0,2},{1,3},{2,0},{3,1},{4,6},{5,7},{6,4},{7,5},{8,10},{9,11},{10,... | collective-permute-start | bytes 786440 | tf_op jit(solution)/shard_map/ppermute | solution.py:121
  78.6 2.0 %fusion.46 = f32[256,2048]{1,0:T(8,128)S(1)} fusion(bf16[768,2048]{1,0:T(8,128)(2,1)S(1)} %multiply_convert_fusion.3, bf16[768,1024]{1,0:T(8,128)(2,1)} %fusion.19, s32[]{:T(128)S(6)} %select_n.23), kind=kOutput, calls=%fused_computation.61 | convolution fusion | flops 805306368 | bytes 5636100 | tf_op jit(solution)/shard_map/rh,rk->hk/dot_general | solution.py:108
  80.6 0.4 fusion.38
  81.0 54.3 %collective-permute-done.3 = bf16[512,256]{1,0:T(8,128)(2,1)S(1)} collective-permute-done((bf16[512,256]{1,0:T(8,128)(2,1)S(1)}, bf16[512,256]{1,0:T(8,128)(2,1)S(1)}, u32[]{:S(2)}, u32[]{:S(2)}) %collective-permute-start.3) | collective-permute-done | bytes 262176 | tf_op jit(solution)/shard_map/ppermute | solution.py:121
  135.3 1.2 fusion.25
  136.5 0.0 collective-permute-done.2
  136.5 3.4 %fusion.12 = f32[1,256,2048]{2,1,0:T(8,128)} fusion(f32[256,2048]{1,0:T(8,128)S(1)} %fusion.46, bf16[768,2048]{1,0:T(8,128)(2,1)S(1)} %multiply_convert_fusion, bf16[256,2048]{1,0:T(8,128)(2,1)S(1)} %collective-permute-done.2, bf16[768,1024]{1,0:T(8,128)(2,1)} %collective-permute-done, s32[]{:T(128)S(6)} %select_n.23), kind=kOutput, calls=%fused_computation.26 | convolution fusion | flops 806879232 | bytes 8781828 | tf_op jit(solution)/shard_map/rh,rk->hk/dot_general | solution.py:108
  (4 shorter events, 0.0 us)
Async XLA Ops:
  0.6 3.8 %copy-start = (bf16[1,2048,256]{2,1,0:T(8,128)(2,1)S(1)}, bf16[1,2048,256]{2,1,0:T(8,128)(2,1)}, u32[]{:S(2)}) copy-start(bf16[1,2048,256]{2,1,0:T(8,128)(2,1)} %param.11) | copy-start | bytes 3145732
  4.2 7.2 %copy-start.7 = (s32[1,2048]{1,0:T(1,128)S(1)}, s32[1,2048]{1,0:T(1,128)}, u32[]{:S(2)}) copy-start(s32[1,2048]{1,0:T(1,128)} %param.8) | copy-start | bytes 24580
  4.2 35.6 %collective-permute-start = (bf16[768,1024]{1,0:T(8,128)(2,1)}, bf16[768,1024]{1,0:T(8,128)(2,1)}, u32[]{:S(2)}, u32[]{:S(2)}) collective-permute-start(bf16[768,1024]{1,0:T(8,128)(2,1)} %fusion.19), channel_id=1, source_target_pairs={{0,1},{1,0},{2,3},{3,2},{4,5},{5,4},{6,7},{7,6},{8,9},{9,8},{10,11... | collective-permute-start | bytes 4718600 | tf_op jit(solution)/shard_map/ppermute | solution.py:55
  11.5 7.1 %copy-start.5 = (bf16[1024]{0:T(1024)(128)(2,1)S(1)}, bf16[1024]{0:T(1024)(128)(2,1)}, u32[]{:S(2)}) copy-start(bf16[1024]{0:T(1024)(128)(2,1)} %param.13) | copy-start | bytes 6148
  11.5 7.1 %copy-start.6 = (s32[256,1]{0,1:T(1,128)S(1)}, s32[256,1]{0,1:T(1,128)}, u32[]{:S(2)}) copy-start(s32[256,1]{0,1:T(1,128)} %param.9) | copy-start | bytes 3076
  13.7 18.8 %all-to-all-start = ((bf16[8,256,256]{2,1,0:T(8,128)(2,1)}), bf16[8,256,256]{2,1,0:T(8,128)(2,1)S(1)}, u32[]{:S(2)}, u32[]{:S(2)}) async-start(bf16[8,256,256]{2,1,0:T(8,128)(2,1)} %bitcast.4), calls=%async_computation | async-start | bytes 2097152 | tf_op jit(solution)/shard_map/all_to_all | solution.py:76
  29.1 4.5 %copy-start.4 = (bf16[64,1024]{1,0:T(8,128)(2,1)S(1)}, bf16[64,1024]{1,0:T(8,128)(2,1)}, u32[]{:S(2)}) copy-start(bf16[64,1024]{1,0:T(8,128)(2,1)} %param.12) | copy-start | bytes 393220
  41.0 19.3 %all-to-all-start.1 = ((bf16[8,256,256]{2,1,0:T(8,128)(2,1)}), bf16[8,256,256]{2,1,0:T(8,128)(2,1)S(1)}, u32[]{:S(2)}, u32[]{:S(2)}) async-start(bf16[8,256,256]{2,1,0:T(8,128)(2,1)} %copy.31), calls=%async_computation.1 | async-start | bytes 2097152 | tf_op jit(solution)/shard_map/all_to_all | solution.py:80
  60.2 2.2 %copy-start.1 = (bf16[768,2048]{1,0:T(8,128)(2,1)S(1)}, bf16[768,2048]{1,0:T(8,128)(2,1)}, u32[]{:S(2)}) copy-start(bf16[768,2048]{1,0:T(8,128)(2,1)} %get-tuple-element.16) | copy-start | bytes 9437188
  62.2 1.9 %copy-start.8 = (bf16[768,2048]{1,0:T(8,128)(2,1)S(1)}, bf16[768,2048]{1,0:T(8,128)(2,1)}, u32[]{:S(2)}) copy-start(bf16[768,2048]{1,0:T(8,128)(2,1)} %get-tuple-element.19) | copy-start | bytes 9437188
  62.2 10.3 %collective-permute-start.1 = (bf16[768,256]{1,0:T(8,128)(2,1)S(1)}, bf16[768,256]{1,0:T(8,128)(2,1)S(1)}, u32[]{:S(2)}, u32[]{:S(2)}) collective-permute-start(bf16[768,256]{1,0:T(8,128)(2,1)S(1)} %get-tuple-element.25), channel_id=1, source_target_pairs={{0,1},{1,0},{2,3},{3,2},{4,5},{5,4},{6,7},{7,6},{8,9},{9,8},{10,11... | collective-permute-start | bytes 1179656 | tf_op jit(solution)/shard_map/ppermute | solution.py:87
  64.5 7.9 %copy-start.2 = (bf16[768,2048]{1,0:T(8,128)(2,1)S(1)}, bf16[768,2048]{1,0:T(8,128)(2,1)}, u32[]{:S(2)}) copy-start(bf16[768,2048]{1,0:T(8,128)(2,1)} %get-tuple-element.18) | copy-start | bytes 9437188
  73.5 2.3 %copy-start.3 = (bf16[768,2048]{1,0:T(8,128)(2,1)S(1)}, bf16[768,2048]{1,0:T(8,128)(2,1)}, u32[]{:S(2)}) copy-start(bf16[768,2048]{1,0:T(8,128)(2,1)} %get-tuple-element.20) | copy-start | bytes 9437188
  75.7 60.8 %collective-permute-start.2 = (bf16[256,2048]{1,0:T(8,128)(2,1)S(1)}, bf16[256,2048]{1,0:T(8,128)(2,1)S(1)}, u32[]{:S(2)}, u32[]{:S(2)}) collective-permute-start(bf16[256,2048]{1,0:T(8,128)(2,1)S(1)} %fusion.13), channel_id=1, source_target_pairs={{0,2},{1,3},{2,0},{3,1},{4,6},{5,7},{6,4},{7,5},{8,10},{9,11},{10,... | collective-permute-start | bytes 3145736 | tf_op jit(solution)/shard_map/ppermute | solution.py:119
  76.2 59.1 %collective-permute-start.3 = (bf16[512,256]{1,0:T(8,128)(2,1)S(1)}, bf16[512,256]{1,0:T(8,128)(2,1)S(1)}, u32[]{:S(2)}, u32[]{:S(2)}) collective-permute-start(bf16[512,256]{1,0:T(8,128)(2,1)S(1)} %fusion.26), channel_id=1, source_target_pairs={{0,2},{1,3},{2,0},{3,1},{4,6},{5,7},{6,4},{7,5},{8,10},{9,11},{10,... | collective-permute-start | bytes 786440 | tf_op jit(solution)/shard_map/ppermute | solution.py:121

commit v5 on v4

--- a/solution.py
+++ b/solution.py
@@ -121,6 +121,7 @@
         seconds.append(lax.ppermute(second_out, "samp", pairs))
     share_first = first_part(near, samp_at) + first_part(far, samp_at)
     share_second = second_part(near, samp_at) + second_part(far, samp_at)
+    share_first, share_second = lax.optimization_barrier((share_first, share_second))
     for arrived in firsts:
         share_first = share_first + arrived.astype(jnp.float32)
     for arrived in seconds:

time: 140 us -> 138 us (0.986)
  other arithmetic: 3.61 us -> 6.08 us
  waiting for transfers between devices: 68.1 us -> 65.7 us
  matrix products: 50.2 us -> 48.1 us
    broadcast_in_dim x0 -> x2, other arithmetic: none -> 2.47 us  [local(): return (row_grads[None], share_first[None], share_second[None])]
    ppermute x1, waiting for transfers between devices: 5.79 us -> 3.36 us  [local(): row_delta_far = lax.ppermute(row_delta, 'samp', across)]
  transfers between devices with their start and end apart: 6 -> 6, of which waited for: 5 -> 5; matrix products, arithmetic and copies ran while one was open for 31% -> 33% of each run, Pallas kernels for 0% -> 0%
where the time goes in v5:
time: 138 us
  waiting for transfers between devices  65.7 us (48%)
  matrix products  48.1 us (35%)
  starting transfers between devices  13.1 us (9%)
  other arithmetic  6.08 us (4%)
  local copies, waits for them, and re-layouts  4.02 us (3%)
    ppermute x1, waiting for transfers between devices, local(): seconds.append(lax.ppermute(second_out, 'samp', pairs))  54.3 us
    dot_general x1, matrix products, hidden_of(): first_pre = jnp.dot(codes, weight_first, preferred_element_type=jnp.float32)  10.4 us
    dot_general x1, matrix products, local(): jnp.dot(encoded_far, weight_first, preferred_element_type=jnp.float32)  10.4 us
    dot_general x4, matrix products, first_part(): jnp.einsum('rh,rk->hk', columns, group[3], preferred_element_type=jnp.flo...  8.29 us
    dot_general x1, matrix products, local(): jnp.dot(hidden_of(encoded)[0], weight_second, preferred_element_type=jnp....  7.03 us
    all_to_all x1, starting transfers between devices, local(): lax.all_to_all(emb_delta, 'feat', split_axis=0, concat_axis=0, tiled=True)  5.44 us
    all_to_all x1, starting transfers between devices, local(): lax.all_to_all(chosen_rows, 'feat', split_axis=0, concat_axis=0, tiled=True)  4.85 us
    convert_element_type x1, other arithmetic, local(): (hash_codes[0].astype(jnp.float32) * (2.0 / (BUCKETS - 1)) - 1.0).astype(...  3.59 us
  transfers between devices with their start and end apart: 6, of which 5 were waited for; matrix products, arithmetic and copies ran while one was open for 33% of the time, Pallas kernels for 0%

profile of v5, /device:TPU:27, one launch (start us, length us, event | category | flops | bytes accessed | tf_op | source)
XLA Modules:
  0.0 137.8 jit_solution(744680297982544900)
XLA Ops:
  0.6 0.0 copy-start
  0.6 3.6 %fusion.17 = bf16[768,1024]{1,0:T(8,128)(2,1)} fusion(s32[1,768,1024]{2,1,0:T(8,128)} %param.7), kind=kLoop, calls=%fused_computation.29 | loop fusion | flops 3145728 | bytes 4718592 | tf_op jit(solution)/shard_map/convert_element_type | solution.py:52
  4.2 0.0 copy-start.7
  4.2 0.2 collective-permute-start
  4.4 0.0 copy-done
  4.4 7.0 %fusion.19 = bf16[768,256]{1,0:T(8,128)(2,1)S(1)} fusion(bf16[768,1024]{1,0:T(8,128)(2,1)} %fusion.17, bf16[1,1024,2048]{2,1,0:T(8,128)(2,1)} %param.10, bf16[1,2048,256]{2,1,0:T(8,128)(2,1)S(1)} %copy-done), kind=kOutput, calls=%fused_computation.31 | convolution fusion | flops 4034592768 | bytes 7208960 | tf_op jit(solution)/shard_map/dot_general | solution.py:62
  11.5 0.0 copy-done.7
  11.5 0.0 copy-start.5
  11.5 0.0 copy-start.6
  11.5 2.3 %fusion.12 = bf16[2048,256]{1,0:T(8,128)(2,1)} fusion(bf16[768,256]{1,0:T(8,128)(2,1)S(1)} %fusion.19, s32[2048]{0:T(1024)S(1)} %bitcast.69), kind=kOutput, calls=%fused_computation.26 | convolution fusion | flops 807403520 | bytes 1449984 | tf_op jit(solution)/shard_map/dot_general | solution.py:70
  13.7 4.9 %all-to-all-start = ((bf16[8,256,256]{2,1,0:T(8,128)(2,1)}), bf16[8,256,256]{2,1,0:T(8,128)(2,1)S(1)}, u32[]{:S(2)}, u32[]{:S(2)}) async-start(bf16[8,256,256]{2,1,0:T(8,128)(2,1)} %bitcast.4), calls=%async_computation | async-start | bytes 2097152 | tf_op jit(solution)/shard_map/all_to_all | solution.py:76
  18.6 0.0 copy-done.5
  18.6 0.0 copy-done.6
  18.7 10.4 %multiply_convert_fusion.4 = (bf16[768,2048]{1,0:T(8,128)(2,1)}, bf16[768,2048]{1,0:T(8,128)(2,1)}) fusion(bf16[768,1024]{1,0:T(8,128)(2,1)} %fusion.17, bf16[1,1024,2048]{2,1,0:T(8,128)(2,1)} %param.10), kind=kOutput, calls=%fused_computation.5 | convolution fusion | flops 3236954112 | bytes 12058624 | tf_op jit(solution)/shard_map/dot_general | solution.py:58
  29.1 0.0 copy-start.4
  29.1 3.5 %all-to-all-done = bf16[8,256,256]{2,1,0:T(8,128)(2,1)S(1)} async-done(((bf16[8,256,256]{2,1,0:T(8,128)(2,1)}), bf16[8,256,256]{2,1,0:T(8,128)(2,1)S(1)}, u32[]{:S(2)}, u32[]{:S(2)}) %all-to-all-start) | async-done | bytes 1048608 | tf_op jit(solution)/shard_map/all_to_all | solution.py:76
  32.5 0.7 fusion.27
  33.2 0.4 copy.27
  33.6 0.0 copy-done.4
  33.6 0.3 fusion.45
  33.9 0.4 fusion.37
  34.3 0.6 convolution_bitcast_fusion
  34.9 0.4 copy.29
  35.3 1.3 copy.28
  36.7 2.0 %fusion.18 = bf16[8,256,256]{2,0,1:T(8,128)(2,1)S(1)} fusion(bf16[8,256,256]{2,1,0:T(8,128)(2,1)S(1)} %all-to-all-done, f32[256,8,8]{2,1,0:T(8,128)S(1)} %copy.29, f32[256,8,8]{1,2,0:T(8,128)} %copy.28), kind=kOutput, calls=%fused_computation.30 | convolution fusion | flops 9469952 | bytes 2228224 | tf_op jit(solution)/shard_map/nfh,hne->fne/dot_general | solution.py:35
  38.7 1.1 collective-permute-done
  39.8 1.2 copy.31
  41.0 5.4 %all-to-all-start.1 = ((bf16[8,256,256]{2,1,0:T(8,128)(2,1)}), bf16[8,256,256]{2,1,0:T(8,128)(2,1)S(1)}, u32[]{:S(2)}, u32[]{:S(2)}) async-start(bf16[8,256,256]{2,1,0:T(8,128)(2,1)} %copy.31), calls=%async_computation.1 | async-start | bytes 2097152 | tf_op jit(solution)/shard_map/all_to_all | solution.py:80
  46.4 10.4 %multiply_convert_fusion.1 = (bf16[768,2048]{1,0:T(8,128)(2,1)}, bf16[768,2048]{1,0:T(8,128)(2,1)}) fusion(bf16[768,1024]{1,0:T(8,128)(2,1)} %collective-permute-done, bf16[1,1024,2048]{2,1,0:T(8,128)(2,1)} %param.10), kind=kOutput, calls=%fused_computation.1 | convolution fusion | flops 3236954112 | bytes 12058624 | tf_op jit(solution)/shard_map/dot_general | solution.py:89
  56.8 3.4 %all-to-all-done.1 = bf16[8,256,256]{2,1,0:T(8,128)(2,1)S(1)} async-done(((bf16[8,256,256]{2,1,0:T(8,128)(2,1)}), bf16[8,256,256]{2,1,0:T(8,128)(2,1)S(1)}, u32[]{:S(2)}, u32[]{:S(2)}) %all-to-all-start.1) | async-done | bytes 1048608 | tf_op jit(solution)/shard_map/all_to_all | solution.py:80
  60.2 0.0 copy-start.1
  60.3 2.0 %fusion.61 = (bf16[768,256]{1,0:T(8,128)(2,1)S(1)}, f32[768,256]{1,0:T(8,128)}) fusion(bf16[2048,256]{1,0:T(8,128)(2,1)S(1)} %bitcast.66, s32[2048]{0:T(1024)S(1)} %bitcast.70), kind=kOutput, calls=%fused_computation.79 | convolution fusion | flops 807075840 | bytes 2236416 | tf_op jit(solution)/shard_map/dot_general | solution.py:83
  62.2 0.0 copy-start.8
  62.2 0.2 collective-permute-start.1
  62.4 0.0 copy-done.1
  62.4 1.0 multiply_convert_fusion.3
  63.4 0.7 copy-done.8
  64.1 0.4 fusion.31
  64.5 2.0 %fusion.39 = f32[256,2048]{1,0:T(8,128)S(1)} fusion(bf16[768,2048]{1,0:T(8,128)(2,1)S(1)} %multiply_convert_fusion.3, bf16[768,1024]{1,0:T(8,128)(2,1)} %fusion.17, s32[]{:T(128)S(6)} %select_n.26), kind=kOutput, calls=%fused_computation.56 | convolution fusion | flops 805306368 | bytes 5636100 | tf_op jit(solution)/shard_map/rh,rk->hk/dot_general | solution.py:108
  66.5 0.4 fusion.34
  67.0 0.0 copy-start.2
  67.0 2.1 %fusion.42 = f32[256,2048]{1,0:T(8,128)S(1)} fusion(bf16[768,2048]{1,0:T(8,128)(2,1)S(1)} %multiply_convert_fusion.3, bf16[768,1024]{1,0:T(8,128)(2,1)} %fusion.17, s32[]{:T(128)S(6)} %select_n.23), kind=kOutput, calls=%fused_computation.59 | convolution fusion | flops 805306368 | bytes 5636100 | tf_op jit(solution)/shard_map/rh,rk->hk/dot_general | solution.py:108
  69.1 3.4 %collective-permute-done.1 = bf16[768,256]{1,0:T(8,128)(2,1)S(1)} collective-permute-done((bf16[768,256]{1,0:T(8,128)(2,1)S(1)}, bf16[768,256]{1,0:T(8,128)(2,1)S(1)}, u32[]{:S(2)}, u32[]{:S(2)}) %collective-permute-start.1) | collective-permute-done | bytes 393248 | tf_op jit(solution)/shard_map/ppermute | solution.py:87
  72.5 0.0 copy-done.2
  72.5 1.0 multiply_convert_fusion
  73.5 0.0 copy-start.3
  73.5 2.2 %fusion.11 = bf16[256,2048]{1,0:T(8,128)(2,1)S(1)} fusion(f32[256,2048]{1,0:T(8,128)S(1)} %fusion.39, bf16[768,2048]{1,0:T(8,128)(2,1)S(1)} %multiply_convert_fusion, bf16[768,1024]{1,0:T(8,128)(2,1)} %collective-permute-done, s32[]{:T(128)S(6)} %select_n.26), kind=kOutput, calls=%fused_computation.25 | convolution fusion | flops 806354944 | bytes 6684676 | tf_op jit(solution)/shard_map/rh,rk->hk/dot_general | solution.py:108
  75.7 0.1 collective-permute-start.2
  75.8 0.0 copy-done.3
  75.8 0.4 fusion.22
  76.2 2.4 %collective-permute-start.3 = (bf16[512,256]{1,0:T(8,128)(2,1)S(1)}, bf16[512,256]{1,0:T(8,128)(2,1)S(1)}, u32[]{:S(2)}, u32[]{:S(2)}) collective-permute-start(bf16[512,256]{1,0:T(8,128)(2,1)S(1)} %fusion.22), channel_id=1, source_target_pairs={{0,2},{1,3},{2,0},{3,1},{4,6},{5,7},{6,4},{7,5},{8,10},{9,11},{10,... | collective-permute-start | bytes 786440 | tf_op jit(solution)/shard_map/ppermute | solution.py:121
  78.6 2.0 %convolution_add_fusion.1 = f32[256,2048]{1,0:T(8,128)S(1)} fusion(f32[256,2048]{1,0:T(8,128)S(1)} %fusion.42, bf16[768,2048]{1,0:T(8,128)(2,1)S(1)} %multiply_convert_fusion, bf16[768,1024]{1,0:T(8,128)(2,1)} %collective-permute-done, s32[]{:T(128)S(6)} %select_n.23), kind=kOutput, calls=%fused_computation.24 | convolution fusion | flops 805830656 | bytes 7733252 | tf_op jit(solution)/shard_map/rh,rk->hk/dot_general | solution.py:108
  80.6 0.4 convolution_add_fusion.3
  81.0 54.3 %collective-permute-done.3 = bf16[512,256]{1,0:T(8,128)(2,1)S(1)} collective-permute-done((bf16[512,256]{1,0:T(8,128)(2,1)S(1)}, bf16[512,256]{1,0:T(8,128)(2,1)S(1)}, u32[]{:S(2)}, u32[]{:S(2)}) %collective-permute-start.3) | collective-permute-done | bytes 262176 | tf_op jit(solution)/shard_map/ppermute | solution.py:121
  135.3 0.9 add_bitcast_fusion.1
  136.2 0.0 collective-permute-done.2
  136.2 1.6 %add_bitcast_fusion = f32[1,256,2048]{2,1,0:T(8,128)} fusion(f32[256,2048]{1,0:T(8,128)S(1)} %convolution_add_fusion.1, bf16[256,2048]{1,0:T(8,128)(2,1)S(1)} %collective-permute-done.2), kind=kLoop, calls=%fused_computation.27 | loop fusion | flops 1048576 | bytes 5242880 | tf_op jit(solution)/shard_map/broadcast_in_dim | solution.py:129
  (4 shorter events, 0.0 us)
Async XLA Ops:
  0.6 3.8 %copy-start = (bf16[1,2048,256]{2,1,0:T(8,128)(2,1)S(1)}, bf16[1,2048,256]{2,1,0:T(8,128)(2,1)}, u32[]{:S(2)}) copy-start(bf16[1,2048,256]{2,1,0:T(8,128)(2,1)} %param.11) | copy-start | bytes 3145732
  4.2 7.2 %copy-start.7 = (s32[1,2048]{1,0:T(1,128)S(1)}, s32[1,2048]{1,0:T(1,128)}, u32[]{:S(2)}) copy-start(s32[1,2048]{1,0:T(1,128)} %param.8) | copy-start | bytes 24580
  4.2 35.6 %collective-permute-start = (bf16[768,1024]{1,0:T(8,128)(2,1)}, bf16[768,1024]{1,0:T(8,128)(2,1)}, u32[]{:S(2)}, u32[]{:S(2)}) collective-permute-start(bf16[768,1024]{1,0:T(8,128)(2,1)} %fusion.17), channel_id=1, source_target_pairs={{0,1},{1,0},{2,3},{3,2},{4,5},{5,4},{6,7},{7,6},{8,9},{9,8},{10,11... | collective-permute-start | bytes 4718600 | tf_op jit(solution)/shard_map/ppermute | solution.py:55
  11.5 7.1 %copy-start.5 = (bf16[1024]{0:T(1024)(128)(2,1)S(1)}, bf16[1024]{0:T(1024)(128)(2,1)}, u32[]{:S(2)}) copy-start(bf16[1024]{0:T(1024)(128)(2,1)} %param.13) | copy-start | bytes 6148
  11.5 7.1 %copy-start.6 = (s32[256,1]{0,1:T(1,128)S(1)}, s32[256,1]{0,1:T(1,128)}, u32[]{:S(2)}) copy-start(s32[256,1]{0,1:T(1,128)} %param.9) | copy-start | bytes 3076
  13.7 18.8 %all-to-all-start = ((bf16[8,256,256]{2,1,0:T(8,128)(2,1)}), bf16[8,256,256]{2,1,0:T(8,128)(2,1)S(1)}, u32[]{:S(2)}, u32[]{:S(2)}) async-start(bf16[8,256,256]{2,1,0:T(8,128)(2,1)} %bitcast.4), calls=%async_computation | async-start | bytes 2097152 | tf_op jit(solution)/shard_map/all_to_all | solution.py:76
  29.1 4.5 %copy-start.4 = (bf16[64,1024]{1,0:T(8,128)(2,1)S(1)}, bf16[64,1024]{1,0:T(8,128)(2,1)}, u32[]{:S(2)}) copy-start(bf16[64,1024]{1,0:T(8,128)(2,1)} %param.12) | copy-start | bytes 393220
  41.0 19.3 %all-to-all-start.1 = ((bf16[8,256,256]{2,1,0:T(8,128)(2,1)}), bf16[8,256,256]{2,1,0:T(8,128)(2,1)S(1)}, u32[]{:S(2)}, u32[]{:S(2)}) async-start(bf16[8,256,256]{2,1,0:T(8,128)(2,1)} %copy.31), calls=%async_computation.1 | async-start | bytes 2097152 | tf_op jit(solution)/shard_map/all_to_all | solution.py:80
  60.2 2.2 %copy-start.1 = (bf16[768,2048]{1,0:T(8,128)(2,1)S(1)}, bf16[768,2048]{1,0:T(8,128)(2,1)}, u32[]{:S(2)}) copy-start(bf16[768,2048]{1,0:T(8,128)(2,1)} %get-tuple-element.18) | copy-start | bytes 9437188
  62.2 1.9 %copy-start.8 = (bf16[768,2048]{1,0:T(8,128)(2,1)S(1)}, bf16[768,2048]{1,0:T(8,128)(2,1)}, u32[]{:S(2)}) copy-start(bf16[768,2048]{1,0:T(8,128)(2,1)} %get-tuple-element.21) | copy-start | bytes 9437188
  62.2 10.3 %collective-permute-start.1 = (bf16[768,256]{1,0:T(8,128)(2,1)S(1)}, bf16[768,256]{1,0:T(8,128)(2,1)S(1)}, u32[]{:S(2)}, u32[]{:S(2)}) collective-permute-start(bf16[768,256]{1,0:T(8,128)(2,1)S(1)} %get-tuple-element.29), channel_id=1, source_target_pairs={{0,1},{1,0},{2,3},{3,2},{4,5},{5,4},{6,7},{7,6},{8,9},{9,8},{10,11... | collective-permute-start | bytes 1179656 | tf_op jit(solution)/shard_map/ppermute | solution.py:87
  67.0 5.5 %copy-start.2 = (bf16[768,2048]{1,0:T(8,128)(2,1)S(1)}, bf16[768,2048]{1,0:T(8,128)(2,1)}, u32[]{:S(2)}) copy-start(bf16[768,2048]{1,0:T(8,128)(2,1)} %get-tuple-element.20) | copy-start | bytes 9437188
  73.5 2.3 %copy-start.3 = (bf16[768,2048]{1,0:T(8,128)(2,1)S(1)}, bf16[768,2048]{1,0:T(8,128)(2,1)}, u32[]{:S(2)}) copy-start(bf16[768,2048]{1,0:T(8,128)(2,1)} %get-tuple-element.22) | copy-start | bytes 9437188
  75.7 60.5 %collective-permute-start.2 = (bf16[256,2048]{1,0:T(8,128)(2,1)S(1)}, bf16[256,2048]{1,0:T(8,128)(2,1)S(1)}, u32[]{:S(2)}, u32[]{:S(2)}) collective-permute-start(bf16[256,2048]{1,0:T(8,128)(2,1)S(1)} %fusion.11), channel_id=1, source_target_pairs={{0,2},{1,3},{2,0},{3,1},{4,6},{5,7},{6,4},{7,5},{8,10},{9,11},{10,... | collective-permute-start | bytes 3145736 | tf_op jit(solution)/shard_map/ppermute | solution.py:119
  76.2 59.1 %collective-permute-start.3 = (bf16[512,256]{1,0:T(8,128)(2,1)S(1)}, bf16[512,256]{1,0:T(8,128)(2,1)S(1)}, u32[]{:S(2)}, u32[]{:S(2)}) collective-permute-start(bf16[512,256]{1,0:T(8,128)(2,1)S(1)} %fusion.22), channel_id=1, source_target_pairs={{0,2},{1,3},{2,0},{3,1},{4,6},{5,7},{6,4},{7,5},{8,10},{9,11},{10,... | collective-permute-start | bytes 786440 | tf_op jit(solution)/shard_map/ppermute | solution.py:121
